TPU v7x, 32 devices: a whole 2x2x4 slice. The times are simulated.
32 devices in a mesh: stn: 16 (over z, y, x), chan: 2 (over core).
Axes of the slice: x: 2, y: 2, z: 4, core: 2. Of those that a mesh axis runs over, the one named last changes fastest.
Arguments:
- voltages: bfloat16 [32, 2, 143, 2048], P(('stn', 'chan')), may hold values from -6 to 6
- flags: float32 [16, 128], P('stn'), may hold values from 0 to 1, as said below
- station_row: int32 [16], P('stn'), may hold values from 0 to 15, each once
Outputs:
- visibility: bfloat16 [2048, 32, 32], P(('stn', 'chan'))
Inputs may be any that keep to these rules, and one draw needn't show every extreme that they name: `flags`: 0 marks a flagged spectrum of a station, 1 a fully usable one; some stations have 0 at all 128 spectra. `station_row`: every row pair is given to exactly one station.
All inputs are finite; a program needn't handle non-finite values.
Results may differ from a plain program's by a relative error of at most 0.006.
Values may be sent and summed in bfloat16 or wider, within the bound.
A program may use at most 64 MiB of HBM per device.

v0:
```python
import math

import jax
import jax.numpy as jnp
from jax import lax
from jax.sharding import PartitionSpec as P


def filter_table(taps, lanes):
    total = taps * lanes
    places = jnp.arange(total, dtype=jnp.float32) + 0.5
    window = 0.5 - 0.5 * jnp.cos(2.0 * math.pi * places / total)
    return (jnp.sinc((places - 0.5 * total) / lanes) * window).reshape(taps, lanes)


def dft_tables(length):
    places = jnp.arange(length, dtype=jnp.int32)
    product = places[:, None] * places[None, :] % length
    angle = 2.0 * math.pi * product.astype(jnp.float32) / length
    return (jnp.cos(angle), jnp.sin(angle))


def twiddle_tables(outer, inner):
    product = (
        jnp.arange(outer, dtype=jnp.int32)[:, None]
        * jnp.arange(inner, dtype=jnp.int32)[None, :]
        % (outer * inner)
    )
    angle = 2.0 * math.pi * product.astype(jnp.float32) / (outer * inner)
    return (jnp.cos(angle), jnp.sin(angle))


def contract(form, left, right):
    return jnp.einsum(form, left, right, precision=lax.Precision.HIGHEST)


def channelize(voltages, spectra_count):
    inputs_here = voltages.shape[0]
    lanes = voltages.shape[3]
    taps = voltages.shape[2] - spectra_count + 1
    taps_table = filter_table(taps, lanes)
    real_acc = taps_table[0] * voltages[:, 0, 0:spectra_count, :].astype(jnp.float32)
    imag_acc = taps_table[0] * voltages[:, 1, 0:spectra_count, :].astype(jnp.float32)
    for tap_index in range(1, taps):
        real_acc = real_acc + taps_table[tap_index] * voltages[
            :, 0, tap_index : tap_index + spectra_count, :
        ].astype(jnp.float32)
        imag_acc = imag_acc + taps_table[tap_index] * voltages[
            :, 1, tap_index : tap_index + spectra_count, :
        ].astype(jnp.float32)
    inner = 128
    outer = lanes // inner
    real_grid = real_acc.reshape(inputs_here, spectra_count, outer, inner)
    imag_grid = imag_acc.reshape(inputs_here, spectra_count, outer, inner)
    cos_outer, sin_outer = dft_tables(outer)
    real_mid = contract("gtmn,mk->gtkn", real_grid, cos_outer) + contract(
        "gtmn,mk->gtkn", imag_grid, sin_outer
    )
    imag_mid = contract("gtmn,mk->gtkn", imag_grid, cos_outer) - contract(
        "gtmn,mk->gtkn", real_grid, sin_outer
    )
    cos_twist, sin_twist = twiddle_tables(outer, inner)
    real_twisted = real_mid * cos_twist + imag_mid * sin_twist
    imag_twisted = imag_mid * cos_twist - real_mid * sin_twist
    cos_inner, sin_inner = dft_tables(inner)
    real_out = contract("gtkn,nj->jkgt", real_twisted, cos_inner) + contract(
        "gtkn,nj->jkgt", imag_twisted, sin_inner
    )
    imag_out = contract("gtkn,nj->jkgt", imag_twisted, cos_inner) - contract(
        "gtkn,nj->jkgt", real_twisted, sin_inner
    )
    scale = 1.0 / math.sqrt(lanes)
    stacked = (jnp.stack([real_out, imag_out], axis=3) * scale).astype(jnp.bfloat16)
    return stacked.reshape(lanes, inputs_here, 2 * spectra_count)


def square_products(plain, turned):
    real_part = jnp.einsum("cat,cbt->cab", plain, plain, preferred_element_type=jnp.float32)
    imag_part = jnp.einsum("cat,cbt->cab", plain, turned, preferred_element_type=jnp.float32)
    return (real_part, imag_part)


def on_device(voltages, flags, station_row):
    spectra_count = flags.shape[1]
    inputs_here = voltages.shape[0]
    lanes = voltages.shape[3]
    stn_count = lax.axis_size("stn")
    chan_count = lax.axis_size("chan")
    per_device = lanes // (stn_count * chan_count)
    total_inputs = inputs_here * stn_count * chan_count
    flags_all, rows_all = (
        lax.all_gather(flags, "stn", axis=0, tiled=True),
        lax.all_gather(station_row, "stn", axis=0, tiled=True),
    )
    spectra = channelize(voltages, spectra_count)
    grouped = spectra.reshape(stn_count, chan_count, per_device, inputs_here, 2 * spectra_count)
    order = jnp.argsort(rows_all)
    rows = jnp.arange(total_inputs, dtype=jnp.int32)
    station_of = order[rows // 2]
    source = 2 * station_of + rows % 2
    moved = lax.all_to_all(
        lax.all_to_all(grouped, "stn", split_axis=0, concat_axis=3, tiled=True),
        "chan",
        split_axis=1,
        concat_axis=3,
        tiled=True,
    )
    from_stn = source // (chan_count * inputs_here)
    from_chan = source // inputs_here % chan_count
    within = source % inputs_here
    placed = from_chan * (stn_count * inputs_here) + from_stn * inputs_here + within
    arrived = moved.reshape(per_device, total_inputs, 2, spectra_count)
    weights = jnp.take(flags_all, station_of, axis=0)
    kept = (
        jnp.take(arrived, placed, axis=1).astype(jnp.float32) * weights[None, :, None, :]
    ).astype(jnp.bfloat16)
    plain = kept.reshape(per_device, total_inputs, 2 * spectra_count)
    turned = jnp.concatenate([-kept[:, :, 1], kept[:, :, 0]], axis=-1)
    count = jnp.dot(
        weights, weights.T, preferred_element_type=jnp.float32, precision=lax.Precision.HIGHEST
    )
    denom = jnp.maximum(count, 1.0)
    real_part, imag_part = square_products(plain, turned)
    below = rows[:, None] >= rows[None, :]
    return jnp.where(below[None], real_part / denom, imag_part / denom).astype(jnp.bfloat16)


def solution(mesh):
    placed = (P(("stn", "chan"), None, None, None), P("stn", None), P("stn"))
    return jax.shard_map(
        on_device,
        mesh=mesh,
        in_specs=placed,
        out_specs=P(("stn", "chan"), None, None),
        check_vma=False,
    )
```

profile of v0, /device:TPU:0, one launch (start us, length us, event | category | flops | bytes accessed | tf_op | source)
XLA Modules:
  0.0 156.7 jit_solution(2867612665235519971)
XLA Ops:
  0.0 0.6 fusion.21
  0.7 28.6 %slice_convert_fusion.15 = (f32[1,1,128,2048]{3,1,2,0:T(1,128)S(1)}, f32[1,1,128,2048]{3,1,2,0:T(1,128)S(1)}, f32[1,1,128,2048]{3,1,2,0:T(1,128)S(1)}, f32[1,1,1...) fusion(bf16[1,2,143,2048]{3,1,2,0:T(2,128)(2,1)} %param.3), kind=kLoop, calls=%fused_computation.39 | loop fusion | flops 4980736 | bytes 29884416 | tf_op jit(solution)/shard_map/convert_element_type | solution.py:43
  29.3 14.0 %slice_convert_fusion.1 = (f32[1,1,128,2048]{3,1,2,0:T(1,128)}, f32[1,1,128,2048]{3,1,2,0:T(1,128)}, f32[1,1,128,2048]{3,1,2,0:T(1,128)}, f32[1,1,128,2048]{3,1,...) fusion(bf16[1,2,143,2048]{3,1,2,0:T(2,128)(2,1)S(1)} %copy-done), kind=kLoop, calls=%fused_computation.25 | loop fusion | flops 3407872 | bytes 20447232 | tf_op jit(solution)/shard_map/convert_element_type | solution.py:50
  43.3 0.7 fusion.64
  43.9 0.6 fusion.116
  44.6 3.2 %multiply_add_fusion = f32[128,16,128]{2,1,0:T(8,128)S(1)} fusion(f32[128,16,128]{2,1,0:T(8,128)} %bitcast.164, f32[128,16,128]{2,1,0:T(8,128)} %bitcast.163, f32[128,16,128]{2,1,0:T(8,128)S(1)} %bitcast.137, f32[128,16,128]{2,1,0:T(8,128)S(1)} %bitcast.138, f32[128,16,128]{2,1,0:T(8,128)S(1)} %bitcast.139, f32[128,16,128]{2,1,0:T(8,128)S(1)} %bitcast.140, ...), kind=kLoop, calls=%fused_computation.23 | loop fusion | flops 8126464 | bytes 17956864 | tf_op jit(solution)/shard_map/add | solution.py:48
  47.9 1.0 fusion.54
  49.4 5.6 %multiply_add_fusion.1 = f32[128,16,128]{2,1,0:T(8,128)S(1)} fusion(f32[128,16,128]{2,1,0:T(8,128)S(1)} %bitcast.131, f32[128,16,128]{2,1,0:T(8,128)S(1)} %bitcast.132, f32[128,16,128]{2,1,0:T(8,128)S(1)} %bitcast.133, f32[128,16,128]{2,1,0:T(8,128)S(1)} %bitcast.134, f32[128,16,128]{2,1,0:T(8,128)S(1)} %bitcast.135, f32[128,16,128]{2,1,0:T(8,128)S(1)} %bitcast.152, ...), kind=kLoop, calls=%fused_computation.40 | loop fusion | flops 8126464 | bytes 17956864 | tf_op jit(solution)/shard_map/add | solution.py:45
  55.0 1.0 fusion.56
  56.0 1.1 fusion.3
  57.1 1.3 add_bitcast_fusion
  58.5 1.4 fusion.13
  59.9 1.4 fusion.9
  61.4 1.5 fusion.2
  62.9 1.7 %fusion.1 = f32[128,16,1,1,128]{4,0,1,3,2:T(8,128)S(1)} fusion(f32[128,128,16]{1,0,2:T(8,128)S(1)} %fusion.9, f32[128,16,128]{2,1,0:T(8,128)S(1)} %get-tuple-element.7), kind=kOutput, calls=%fused_computation.8 | convolution fusion | flops 403144704 | bytes 3145728 | tf_op jit(solution)/shard_map/gtkn,nj->jkgt/dot_general | solution.py:34
  64.9 1.1 copy.37
  66.0 1.5 convert_element_type.489
  67.5 8.4 %all-to-all-start = ((bf16[16,2,64,1,256]{4,2,1,3,0:T(8,128)(2,1)}), bf16[16,2,64,1,256]{4,2,1,3,0:T(8,128)(2,1)S(1)}, u32[]{:S(2)}, u32[]{:S(2)}) async-start(bf16[16,2,64,1,256]{4,2,1,3,0:T(8,128)(2,1)} %bitcast.52), calls=%async_computation | async-start | bytes 2097152 | tf_op jit(solution)/shard_map/all_to_all | solution.py:102
  77.2 0.8 dynamic-update-slice
  77.9 23.9 %all-reduce = s32[16]{0:T(128)S(1)} all-reduce(s32[16]{0:T(128)S(1)} %dynamic-update-slice), channel_id=1, replica_groups=mesh['stn'=16,'chan'=2] {'stn'}, use_global_device_ids=true, to_apply=%add | all-reduce | flops 16 | bytes 128
  101.8 1.2 sort.17
  103.0 0.7 gather_fusion
  103.7 38.5 %all-gather = f32[16,1,128]{2,1,0:T(1,128)S(1)} all-gather(f32[1,1,128]{2,1,0:T(1,128)S(1)} %bitcast.169), channel_id=1, replica_groups=mesh['stn'=16,'chan'=2] {'stn'}, dimensions={0}, use_global_device_ids=true | all-gather | bytes 8704 | tf_op jit(solution)/shard_map/all_gather | solution.py:92
  143.2 4.6 %all_to_all.33 = bf16[1,2,64,16,256]{4,2,3,0,1:T(8,128)(2,1)S(1)} all-to-all(bf16[1,2,64,16,256]{4,2,3,0,1:T(8,128)(2,1)S(1)} %copy.39), channel_id=1, replica_groups=mesh['stn'=16,'chan'=2] {'chan'}, dimensions={1} | all-to-all | bytes 2097152 | tf_op jit(solution)/shard_map/all_to_all | solution.py:101
  148.4 0.8 gather_fusion.1
  149.1 0.7 multiply_convert_fusion
  149.9 1.1 fusion.15
  151.0 1.1 copy.43
  152.0 0.7 gather.18
  152.8 0.6 fusion.16
  154.5 0.6 copy.45
  155.7 1.0 select_convert_fusion
  (53 shorter events, 4.5 us)
Async XLA Ops:
  0.6 28.7 %copy-start = (bf16[1,2,143,2048]{3,1,2,0:T(2,128)(2,1)S(1)}, bf16[1,2,143,2048]{3,1,2,0:T(2,128)(2,1)}, u32[]{:S(2)}) copy-start(bf16[1,2,143,2048]{3,1,2,0:T(2,128)(2,1)} %param.3) | copy-start | bytes 3514372
  47.8 1.2 copy-start.1
  47.8 1.5 copy-start.2
  47.8 1.5 copy-start.5
  47.8 1.5 copy-start.6
  47.8 1.5 copy-start.7
  47.8 1.5 copy-start.8
  47.9 1.5 copy-start.9
  47.9 1.5 copy-start.10
  47.9 1.5 copy-start.11
  56.0 1.1 copy-start.12
  56.0 1.1 copy-start.13
  67.5 9.1 %copy-start.15 = (u32[32]{0:T(128)S(1)}, u32[32]{0:T(128)}, u32[]{:S(2)}) copy-start(u32[32]{0:T(128)} %constant.248) | copy-start | bytes 388
  67.5 36.3 %copy-start.14 = (f32[1,128]{1,0:T(1,128)S(1)}, f32[1,128]{1,0:T(1,128)}, u32[]{:S(2)}) copy-start(f32[1,128]{1,0:T(1,128)} %param.4) | copy-start | bytes 1540
  67.5 75.6 %all-to-all-start = ((bf16[16,2,64,1,256]{4,2,1,3,0:T(8,128)(2,1)}), bf16[16,2,64,1,256]{4,2,1,3,0:T(8,128)(2,1)S(1)}, u32[]{:S(2)}, u32[]{:S(2)}) async-start(bf16[16,2,64,1,256]{4,2,1,3,0:T(8,128)(2,1)} %bitcast.52), calls=%async_computation | async-start | bytes 2097152 | tf_op jit(solution)/shard_map/all_to_all | solution.py:102
  152.8 1.0 copy-start.3
  152.8 1.2 copy-start.4
where the time goes:
time: 157 us
  blocking collectives  66.9 us (43%)
  other arithmetic  57.3 us (36%)
  matrix products  11.8 us (8%)
  local copies, waits for them, and re-layouts  11.2 us (7%)
  starting transfers between devices  8.43 us (5%)
    all_gather x1, blocking collectives, on_device(): lax.all_gather(flags, 'stn', axis=0, tiled=True)  38.5 us
    convert_element_type x1, other arithmetic, channelize(): voltages[:, 1, 0:spectra_count, :].astype(jnp.float32)  28.6 us
    unnamed x1, blocking collectives  23.9 us
    convert_element_type x1, other arithmetic, channelize(): imag_acc = imag_acc + taps_table[tap_index] * voltages[:, 1, tap_index:ta...  14 us
    dot_general x8, matrix products, contract(): return jnp.einsum(form, left, right, precision=lax.Precision.HIGHEST)  10.6 us
    all_to_all x1, starting transfers between devices, on_device(): lax.all_to_all(grouped, 'stn', split_axis=0, concat_axis=3, tiled=True)  8.43 us
    add x1, other arithmetic, channelize(): real_acc + taps_table[tap_index] * voltages[:, 0, tap_index:tap_index + s...  5.58 us
    all_to_all x1, blocking collectives, on_device(): lax.all_to_all(lax.all_to_all(grouped, 'stn', split_axis=0, concat_axis=3...  4.58 us
  transfers between devices with their start and end apart: 1, of which 0 were waited for; matrix products, arithmetic and copies ran while one was open for 3% of the time, Pallas kernels for 0%

commit v1 on v0

--- a/solution.py
+++ b/solution.py
@@ -1,9 +1,16 @@
+import functools
 import math
 
 import jax
 import jax.numpy as jnp
+import numpy as np
 from jax import lax
+from jax.experimental import pallas as pl
+from jax.experimental.pallas import tpu as pltpu
 from jax.sharding import PartitionSpec as P
+
+LANES = 128
+ROWS = 8
 
 
 def filter_table(taps, lanes):
@@ -88,6 +95,14 @@
     chan_count = lax.axis_size("chan")
     per_device = lanes // (stn_count * chan_count)
     total_inputs = inputs_here * stn_count * chan_count
+    if (
+        total_inputs == 32
+        and inputs_here == 1
+        and chan_count == 2
+        and lanes == 16 * LANES
+        and spectra_count == LANES
+    ):
+        return fused(voltages, flags, station_row, stn_count, chan_count)
     flags_all, rows_all = (
         lax.all_gather(flags, "stn", axis=0, tiled=True),
         lax.all_gather(station_row, "stn", axis=0, tiled=True),
@@ -125,6 +140,315 @@
     return jnp.where(below[None], real_part / denom, imag_part / denom).astype(jnp.bfloat16)
 
 
+def host_tables(taps, lanes, devices):
+    outer = lanes // LANES
+    quads = LANES // devices
+    total = taps * lanes
+    places = np.arange(total) + 0.5
+    window = 0.5 - 0.5 * np.cos(2.0 * np.pi * places / total)
+    taper = (np.sinc((places - 0.5 * total) / lanes) * window).reshape(taps, outer, LANES)
+    taper = taper.transpose(1, 0, 2)
+    angle = 2.0 * np.pi * (np.arange(outer)[:, None] * np.arange(LANES)[None, :]) / lanes
+    scale = 1.0 / math.sqrt(lanes)
+    twist = np.stack([np.cos(angle), np.sin(angle)]) * scale
+    turn = 2.0 * np.pi * (np.arange(LANES)[:, None] * np.arange(LANES)[None, :] % LANES) / LANES
+    cos, sin = np.cos(turn), np.sin(turn)
+    real_rows = np.concatenate([cos, sin], axis=1).reshape(devices, 1, quads, 2 * LANES)
+    imag_rows = np.concatenate([-sin, cos], axis=1).reshape(devices, 1, quads, 2 * LANES)
+    matrix = np.concatenate([real_rows, imag_rows], axis=1).reshape(2 * LANES, 2 * LANES)
+    return (
+        jnp.asarray(taper.astype(np.float32)),
+        jnp.asarray(twist.astype(np.float32)),
+        jnp.asarray(matrix.astype(np.float32)).astype(jnp.bfloat16),
+    )
+
+
+def dft4(a, b, c, d):
+    s0 = (a[0] + c[0], a[1] + c[1])
+    s1 = (a[0] - c[0], a[1] - c[1])
+    s2 = (b[0] + d[0], b[1] + d[1])
+    s3 = (b[0] - d[0], b[1] - d[1])
+    return (
+        (s0[0] + s2[0], s0[1] + s2[1]),
+        (s1[0] + s3[1], s1[1] - s3[0]),
+        (s0[0] - s2[0], s0[1] - s2[1]),
+        (s1[0] - s3[1], s1[1] + s3[0]),
+    )
+
+
+def dft16(x):
+    half = math.sqrt(0.5)
+    mids = [dft4(x[p], x[4 + p], x[8 + p], x[12 + p]) for p in range(4)]
+    out = [None] * 16
+    for kx in range(4):
+        turned = []
+        for p in range(4):
+            re, im = mids[p][kx]
+            e = p * kx
+            if e == 0:
+                turned.append((re, im))
+            elif e == 4:
+                turned.append((im, -re))
+            elif e == 2:
+                turned.append(((re + im) * half, (im - re) * half))
+            elif e == 6:
+                turned.append(((im - re) * half, -(re + im) * half))
+            else:
+                c, s = math.cos(2 * math.pi * e / 16), math.sin(2 * math.pi * e / 16)
+                turned.append((re * c + im * s, im * c - re * s))
+        for ky, value in enumerate(dft4(*turned)):
+            out[kx + 4 * ky] = value
+    return out
+
+
+def iota(shape, dim):
+    return lax.broadcasted_iota(jnp.int32, shape, dim)
+
+
+def kernel(
+    stn_count, chan_count, chunks,
+    volt_hbm, flags_ref, row_ref, taper_ref, twist_ref, matrix_ref, out_ref,
+    volt, wide, filt, mids, send, recv, meta, gathered, acc,
+    load_sem, send_sem, recv_sem, meta_send_sem, meta_recv_sem,
+):
+    devices = stn_count * chan_count
+    outer, taps = taper_ref.shape[0], taper_ref.shape[1]
+    frames = volt.shape[1]
+    spectra = flags_ref.shape[1]
+    span = spectra // chunks
+    packed = LANES // span
+    groups = outer // packed
+    quads = LANES // devices
+    block = groups * ROWS
+    stn, chan = lax.axis_index("stn"), lax.axis_index("chan")
+    me = stn * chan_count + chan
+    bits = devices.bit_length() - 1
+
+    load = pltpu.make_async_copy(volt_hbm.at[0], volt, load_sem)
+    load.start()
+
+    def partner(step):
+        other = jnp.int32(0)
+        for bit in range(bits):
+            other = other + ((me // 2**bit + step // 2**bit) % 2) * 2**bit
+        return other
+
+    barrier = pltpu.get_barrier_semaphore()
+
+    def greet(step, carry):
+        other = partner(step)
+        pl.semaphore_signal(
+            barrier, inc=1, device_id=(other // chan_count, other % chan_count),
+            device_id_type=pl.DeviceIdType.MESH,
+        )
+        return carry
+
+    lax.fori_loop(1, devices, greet, 0)
+
+    flags8 = jnp.broadcast_to(flags_ref[...], (ROWS, LANES))
+    station = jnp.broadcast_to(row_ref[0], (ROWS, LANES)).astype(jnp.float32)
+    meta[stn] = jnp.where(iota((ROWS, LANES), 0) == 0, flags8, station)
+
+    def meta_copy(other):
+        return pltpu.make_async_remote_copy(
+            src_ref=meta.at[stn], dst_ref=meta.at[stn],
+            send_sem=meta_send_sem, recv_sem=meta_recv_sem,
+            device_id=(other, chan), device_id_type=pl.DeviceIdType.MESH,
+        )
+
+    def block_copy(chunk, other):
+        return pltpu.make_async_remote_copy(
+            src_ref=send.at[chunk, other], dst_ref=recv.at[chunk, me],
+            send_sem=send_sem.at[chunk], recv_sem=recv_sem.at[chunk],
+            device_id=(other // chan_count, other % chan_count),
+            device_id_type=pl.DeviceIdType.MESH,
+        )
+
+    load.wait()
+    lane8 = iota((ROWS, LANES), 1)
+    for chunk in range(chunks):
+        start = chunk * span
+        low = 0 if chunk == 0 else start + taps
+        high = min(start + span + taps, frames)
+
+        def widen(a, carry, low=low, high=high):
+            lanes = pl.ds(pl.multiple_of(a * LANES, LANES), LANES)
+            for part in range(2):
+                wide[part, a, low:high, :] = volt[part, low:high, lanes].astype(jnp.float32)
+            return carry
+
+        lax.fori_loop(0, outer, widen, 0)
+
+        def fir(a, carry, start=start):
+            for part in range(2):
+                total = taper_ref[a, 0:1, :] * wide[part, a, start : start + span, :]
+                for tap in range(1, taps):
+                    total = total + taper_ref[a, tap : tap + 1, :] * wide[
+                        part, a, start + tap : start + tap + span, :
+                    ]
+                filt[part, a] = total
+            return carry
+
+        lax.fori_loop(0, outer, fir, 0)
+
+        def first_stage(tile, carry):
+            rows = pl.ds(pl.multiple_of(tile * ROWS, ROWS), ROWS)
+            values = dft16([(filt[0, a, rows, :], filt[1, a, rows, :]) for a in range(outer)])
+            for k in range(outer):
+                re, im = values[k]
+                c, s = twist_ref[0, k : k + 1, :], twist_ref[1, k : k + 1, :]
+                mids[k, rows, 0:LANES] = re * c + im * s
+                mids[k, rows, LANES:] = im * c - re * s
+            return carry
+
+        lax.fori_loop(0, span // ROWS, first_stage, 0)
+
+        weights8 = jnp.zeros((ROWS, LANES), jnp.float32)
+        for j in range(packed):
+            shift = (span * j - start) % LANES
+            rolled = pltpu.roll(flags8, shift, 1) if shift else flags8
+            weights8 = jnp.where(lane8 // span == j, rolled, weights8)
+        for pair in range(groups // 2):
+            halves = []
+            for group in (2 * pair, 2 * pair + 1):
+                data = mids[packed * group : packed * (group + 1)].reshape(LANES, 2 * LANES)
+                spectrum = lax.dot_general(
+                    matrix_ref[...], data.astype(jnp.bfloat16), (((1,), (1,)), ((), ())),
+                    preferred_element_type=jnp.float32,
+                )
+                rounded = spectrum.astype(jnp.bfloat16).astype(jnp.float32)
+                halves.append(rounded.reshape(devices, ROWS, LANES) * weights8[None])
+            send[chunk, :, 2 * ROWS * pair : 2 * ROWS * (pair + 1), :] = jnp.concatenate(
+                halves, axis=1
+            ).astype(jnp.bfloat16)
+
+        if chunk == 0:
+            pl.semaphore_wait(barrier, devices - 1)
+
+            def tell(step, carry):
+                meta_copy((stn + step) % stn_count).start()
+                return carry
+
+        def push(step, carry, chunk=chunk):
+            block_copy(chunk, partner(devices - step)).start()
+            return carry
+
+        lax.fori_loop(1, devices, push, 0)
+        if chunk == 0:
+            lax.fori_loop(1, stn_count, tell, 0)
+        recv[chunk, me] = send[chunk, me]
+
+    lane = iota((devices, 2 * LANES), 1) % LANES // span
+    for chunk in range(chunks):
+        arrived = recv.at[chunk, pl.ds(0, devices - 1)]
+        pltpu.make_async_copy(arrived, arrived, recv_sem.at[chunk]).wait()
+        gathered[...] = recv[chunk].reshape(devices * block, LANES).astype(jnp.float32)
+        for quad in range(quads):
+            for group in range(groups):
+                at = group * ROWS + quad
+                re = gathered[pl.ds(at, devices, stride=block), :].astype(jnp.bfloat16)
+                im = gathered[pl.ds(at + quads, devices, stride=block), :].astype(jnp.bfloat16)
+                plain = jnp.concatenate([re, im], axis=1)
+                turned = jnp.concatenate([im, -re], axis=1)
+                left = jnp.concatenate([plain, turned], axis=0)
+                zero = jnp.zeros_like(plain)
+                right = jnp.concatenate(
+                    [jnp.where(lane == j, plain, zero) for j in range(packed)], axis=0
+                )
+                product = lax.dot_general(
+                    left, right, (((1,), (1,)), ((), ())), preferred_element_type=jnp.float32
+                )
+                if chunk == 0:
+                    acc[quad * groups + group] = product
+                else:
+                    acc[quad * groups + group] += product
+
+    told = meta.at[pl.ds(0, stn_count - 1)]
+    pltpu.make_async_copy(told, told, meta_recv_sem).wait()
+    tall = packed * devices
+    exact = functools.partial(
+        lax.dot_general, precision=lax.Precision.HIGHEST, preferred_element_type=jnp.float32
+    )
+    spread = (iota((tall, stn_count), 0) % devices // 2 == iota((tall, stn_count), 1)).astype(
+        jnp.float32
+    )
+    all_flags = meta[:, 0, :]
+    all_rows = meta[:, 1, :]
+    weights = exact(spread, all_flags, (((1,), (0,)), ((), ())))
+    count = exact(weights[:devices], weights, (((1,), (1,)), ((), ())))
+    place = 2 * exact(spread, all_rows, (((1,), (0,)), ((), ()))).astype(jnp.int32)
+    place = place + iota(place.shape, 0) % 2
+    across = place.T
+    lower = place[:devices] >= across[:devices]
+    denom = jnp.maximum(count, 1.0)
+    lane_at = iota((tall, tall), 1)
+    columns = jnp.logical_and(
+        place == lane_at % devices, iota((tall, tall), 0) // devices == lane_at // devices
+    ).astype(jnp.bfloat16)
+    row_of = (across[:devices, :devices] == iota((devices, devices), 0)).astype(jnp.bfloat16)
+    for g in range(quads * groups):
+        both = acc[g]
+        chosen = jnp.where(lower, both[:devices], both[devices:]) / denom
+        moved = jnp.dot(chosen.astype(jnp.bfloat16), columns, preferred_element_type=jnp.float32)
+        moved = jnp.dot(
+            row_of, moved.astype(jnp.bfloat16), preferred_element_type=jnp.float32
+        ).astype(jnp.bfloat16)
+        for j in range(packed):
+            out_ref[packed * g + j] = moved[:, devices * j : devices * (j + 1)]
+
+    for chunk in range(chunks):
+        gone = send.at[chunk, pl.ds(0, devices - 1)]
+        pltpu.make_async_copy(gone, gone, send_sem.at[chunk]).wait()
+    pltpu.make_async_copy(told, told, meta_send_sem).wait()
+
+
+def fused(voltages, flags, station_row, stn_count, chan_count):
+    devices = stn_count * chan_count
+    frames, lanes = voltages.shape[2], voltages.shape[3]
+    spectra = flags.shape[1]
+    taps = frames - spectra + 1
+    outer = lanes // LANES
+    chunks = 4
+    span = spectra // chunks
+    packed = LANES // span
+    block = outer // packed * ROWS
+    taper, twist, matrix = host_tables(taps, lanes, devices)
+    vmem = pl.BlockSpec(memory_space=pltpu.VMEM)
+    f32, bf16 = jnp.float32, jnp.bfloat16
+    return pl.pallas_call(
+        functools.partial(kernel, stn_count, chan_count, chunks),
+        out_shape=jax.ShapeDtypeStruct((lanes // devices, devices, devices), bf16),
+        in_specs=[
+            pl.BlockSpec(memory_space=pl.ANY),
+            vmem,
+            pl.BlockSpec(memory_space=pltpu.SMEM),
+            vmem,
+            vmem,
+            vmem,
+        ],
+        out_specs=vmem,
+        scratch_shapes=[
+            pltpu.VMEM((2, frames, lanes), bf16),
+            pltpu.VMEM((2, outer, frames, LANES), f32),
+            pltpu.VMEM((2, outer, span, LANES), f32),
+            pltpu.VMEM((outer, span, 2 * LANES), f32),
+            pltpu.VMEM((chunks, devices, block, LANES), bf16),
+            pltpu.VMEM((chunks, devices, block, LANES), bf16),
+            pltpu.VMEM((stn_count, ROWS, LANES), f32),
+            pltpu.VMEM((devices * block, LANES), f32),
+            pltpu.VMEM((outer * (LANES // devices) // packed, 2 * devices, packed * devices), f32),
+            pltpu.SemaphoreType.DMA,
+            pltpu.SemaphoreType.DMA((chunks,)),
+            pltpu.SemaphoreType.DMA((chunks,)),
+            pltpu.SemaphoreType.DMA,
+            pltpu.SemaphoreType.DMA,
+        ],
+        compiler_params=pltpu.CompilerParams(
+            collective_id=0, has_side_effects=True, vmem_limit_bytes=32 * 1024 * 1024
+        ),
+    )(voltages, flags, station_row, taper, twist, matrix)
+
+
 def solution(mesh):
     placed = (P(("stn", "chan"), None, None, None), P("stn", None), P("stn"))
     return jax.shard_map(

time: 157 us -> 40.9 us (0.26)
  blocking collectives: 66.9 us -> 0 us
  other arithmetic: 57.3 us -> 0 us
  Pallas kernels: 0 us -> 37.1 us
  matrix products: 11.8 us -> 0 us
  starting transfers between devices: 8.43 us -> 0 us
  local copies, waits for them, and re-layouts: 11.2 us -> 2.97 us
    convert_element_type x5 -> x0, other arithmetic: 44.7 us -> none  [the longest x1 28.6 us: channelize(): voltages[:, 1, 0:spectra_count, :].astype(jnp.float32)]
    all_gather x1 -> x0, blocking collectives: 38.5 us -> none  [on_device(): lax.all_gather(flags, 'stn', axis=0, tiled=True)]
    pallas_call x0 -> x1, Pallas kernels: none -> 37.1 us  [fused(): pl.pallas_call(functools.partial(kernel, stn_count, chan_count, chunks),...]
    unnamed x1 -> x0, blocking collectives: 23.9 us -> none
    dot_general x11 -> x0, matrix products: 11.8 us -> none  [the longest x8 10.6 us: contract(): return jnp.einsum(form, left, right, precision=lax.Precision.HIGHEST)]
    add x2 -> x0, other arithmetic: 8.78 us -> none  [the longest x1 5.58 us: channelize(): real_acc + taps_table[tap_index] * voltages[:, 0, tap_index:tap_index + s...]
    all_to_all x1 -> x0, starting transfers between devices: 8.43 us -> none  [on_device(): lax.all_to_all(grouped, 'stn', split_axis=0, concat_axis=3, tiled=True)]
    all_to_all x1 -> x0, blocking collectives: 4.58 us -> none  [on_device(): lax.all_to_all(lax.all_to_all(grouped, 'stn', split_axis=0, concat_axis=3...]
  transfers between devices with their start and end apart: 1 -> 0, of which waited for: 0 -> 0; matrix products, arithmetic and copies ran while one was open for 3% -> 0% of each run, Pallas kernels for 0% -> 0%
where the time goes in v1:
time: 40.9 us; the launch traced here: 40.8 us
  Pallas kernels  37.1 us (91%)
  local copies, waits for them, and re-layouts  2.97 us (7%)
  between operations  0.74 us (2%)
    pallas_call x1, Pallas kernels, fused(): pl.pallas_call(functools.partial(kernel, stn_count, chan_count, chunks),...  37.1 us
    unnamed x9, local copies, waits for them, and re-layouts  1.7 us
    pallas_call x1, local copies, waits for them, and re-layouts, fused(): pl.pallas_call(functools.partial(kernel, stn_count, chan_count, chunks),...  1.27 us

profile of v1, /device:TPU:0, one launch (start us, length us, event | category | flops | bytes accessed | tf_op | source)
XLA Modules:
  0.0 40.8 jit_solution(14196000312874580378)
XLA Ops:
  0.0 0.0 copy-start
  0.0 0.0 copy-start.2
  0.0 0.0 copy-start.1
  0.0 0.0 copy-start.3
  0.7 1.7 %copy.7.volt_hbm = bf16[1,2,143,2048]{3,2,1,0:T(8,128)(2,1)S(1)} copy(bf16[1,2,143,2048]{3,1,2,0:T(2,128)(2,1)} %param.6) | data formatting | bytes 2342912 | tf_op args[0]
  2.4 0.0 copy-done
  2.4 0.0 copy-done.2
  2.4 0.0 copy-done.1
  2.4 0.0 copy-done.3
  2.4 37.1 %shard_map.64 = bf16[64,32,32]{2,1,0:T(8,128)(2,1)S(1)} custom-call(bf16[1,2,143,2048]{3,2,1,0:T(8,128)(2,1)S(1)} %copy.7.volt_hbm, f32[1,128]{1,0:T(1,128)S(1)} %copy-done.3, s32[1]{0:T(128)S(6)} %copy.9.row_ref, f32[16,16,128]{2,1,0:T(8,128)S(1)} %copy-done.1, f32[2,16,128]{2,1,0:T(8,128)S(1)} %copy-done.2, bf16[256,256]{1,0:T(8,128)(2,1)S(1)} %copy-done), custom_call_target="tpu_custom_call" | custom-call | tf_op jit(solution)/shard_map/pallas_call | solution.py:418
  39.5 1.3 %copy.8 = bf16[64,32,32]{0,2,1:T(8,128)(2,1)} copy(bf16[64,32,32]{2,1,0:T(8,128)(2,1)S(1)} %shard_map.64) | data formatting | bytes 262144 | tf_op jit(solution)/shard_map/pallas_call | solution.py:418
Async XLA Ops:
  0.0 2.4 %copy-start = (bf16[256,256]{1,0:T(8,128)(2,1)S(1)}, bf16[256,256]{1,0:T(8,128)(2,1)}, u32[]{:S(2)}) copy-start(bf16[256,256]{1,0:T(8,128)(2,1)} %constant.12.matrix_ref) | copy-start | bytes 393220
  0.0 2.4 %copy-start.2 = (f32[2,16,128]{2,1,0:T(8,128)S(1)}, f32[2,16,128]{2,1,0:T(8,128)}, u32[]{:S(2)}) copy-start(f32[2,16,128]{2,1,0:T(8,128)} %constant.7.clone.twist_ref) | copy-start | bytes 49156
  0.0 2.4 %copy-start.1 = (f32[16,16,128]{2,1,0:T(8,128)S(1)}, f32[16,16,128]{2,1,0:T(8,128)}, u32[]{:S(2)}) copy-start(f32[16,16,128]{2,1,0:T(8,128)} %constant.6.clone.taper_ref) | copy-start | bytes 393220
  0.0 2.4 %copy-start.3 = (f32[1,128]{1,0:T(1,128)S(1)}, f32[1,128]{1,0:T(1,128)}, u32[]{:S(2)}) copy-start(f32[1,128]{1,0:T(1,128)} %flags_ref.1) | copy-start | bytes 1540

commit v2 on v1

--- a/solution.py
+++ b/solution.py
@@ -330,7 +330,9 @@
                 return carry
 
         def push(step, carry, chunk=chunk):
-            block_copy(chunk, partner(devices - step)).start()
+            far = devices - 1 - (step - 1) // 2
+            near = devices // 2 - step // 2
+            block_copy(chunk, partner(step % 2 * far + (1 - step % 2) * near)).start()
             return carry
 
         lax.fori_loop(1, devices, push, 0)
@@ -338,6 +340,29 @@
             lax.fori_loop(1, stn_count, tell, 0)
         recv[chunk, me] = send[chunk, me]
 
+    told = meta.at[pl.ds(0, stn_count - 1)]
+    pltpu.make_async_copy(told, told, meta_recv_sem).wait()
+    tall = packed * devices
+    exact = functools.partial(
+        lax.dot_general, precision=lax.Precision.HIGHEST, preferred_element_type=jnp.float32
+    )
+    spread = (iota((tall, stn_count), 0) % devices // 2 == iota((tall, stn_count), 1)).astype(
+        jnp.float32
+    )
+    all_flags = meta[:, 0, :]
+    all_rows = meta[:, 1, :]
+    weights = exact(spread, all_flags, (((1,), (0,)), ((), ())))
+    count = exact(weights[:devices], weights, (((1,), (1,)), ((), ())))
+    place = 2 * exact(spread, all_rows, (((1,), (0,)), ((), ()))).astype(jnp.int32)
+    place = place + iota(place.shape, 0) % 2
+    across = place.T
+    lower = place[:devices] >= across[:devices]
+    denom = jnp.maximum(count, 1.0)
+    lane_at = iota((tall, tall), 1)
+    columns = jnp.logical_and(
+        place == lane_at % devices, iota((tall, tall), 0) // devices == lane_at // devices
+    ).astype(jnp.bfloat16)
+    row_of = (across[:devices, :devices] == iota((devices, devices), 0)).astype(jnp.bfloat16)
     lane = iota((devices, 2 * LANES), 1) % LANES // span
     for chunk in range(chunks):
         arrived = recv.at[chunk, pl.ds(0, devices - 1)]
@@ -363,29 +388,6 @@
                 else:
                     acc[quad * groups + group] += product
 
-    told = meta.at[pl.ds(0, stn_count - 1)]
-    pltpu.make_async_copy(told, told, meta_recv_sem).wait()
-    tall = packed * devices
-    exact = functools.partial(
-        lax.dot_general, precision=lax.Precision.HIGHEST, preferred_element_type=jnp.float32
-    )
-    spread = (iota((tall, stn_count), 0) % devices // 2 == iota((tall, stn_count), 1)).astype(
-        jnp.float32
-    )
-    all_flags = meta[:, 0, :]
-    all_rows = meta[:, 1, :]
-    weights = exact(spread, all_flags, (((1,), (0,)), ((), ())))
-    count = exact(weights[:devices], weights, (((1,), (1,)), ((), ())))
-    place = 2 * exact(spread, all_rows, (((1,), (0,)), ((), ()))).astype(jnp.int32)
-    place = place + iota(place.shape, 0) % 2
-    across = place.T
-    lower = place[:devices] >= across[:devices]
-    denom = jnp.maximum(count, 1.0)
-    lane_at = iota((tall, tall), 1)
-    columns = jnp.logical_and(
-        place == lane_at % devices, iota((tall, tall), 0) // devices == lane_at // devices
-    ).astype(jnp.bfloat16)
-    row_of = (across[:devices, :devices] == iota((devices, devices), 0)).astype(jnp.bfloat16)
     for g in range(quads * groups):
         both = acc[g]
         chosen = jnp.where(lower, both[:devices], both[devices:]) / denom

time: 40.9 us -> 40.3 us (0.985)
  Pallas kernels: 37.1 us -> 36.5 us
    pallas_call x1, Pallas kernels: 37.1 us -> 36.5 us  [fused(): pl.pallas_call(functools.partial(kernel, stn_count, chan_count, chunks),...]
where the time goes in v2:
time: 40.3 us; the launch traced here: 40.2 us
  Pallas kernels  36.5 us (91%)
  local copies, waits for them, and re-layouts  2.97 us (7%)
  between operations  0.74 us (2%)
    pallas_call x1, Pallas kernels, fused(): pl.pallas_call(functools.partial(kernel, stn_count, chan_count, chunks),...  36.5 us
    unnamed x9, local copies, waits for them, and re-layouts  1.7 us
    pallas_call x1, local copies, waits for them, and re-layouts, fused(): pl.pallas_call(functools.partial(kernel, stn_count, chan_count, chunks),...  1.27 us

profile of v2, /device:TPU:0, one launch (start us, length us, event | category | flops | bytes accessed | tf_op | source)
XLA Modules:
  0.0 40.2 jit_solution(5889107108440993649)
XLA Ops:
  0.0 0.0 copy-start
  0.0 0.0 copy-start.2
  0.0 0.0 copy-start.1
  0.0 0.0 copy-start.3
  0.7 1.7 %copy.7.volt_hbm = bf16[1,2,143,2048]{3,2,1,0:T(8,128)(2,1)S(1)} copy(bf16[1,2,143,2048]{3,1,2,0:T(2,128)(2,1)} %param.6) | data formatting | bytes 2342912 | tf_op args[0]
  2.4 0.0 copy-done
  2.4 0.0 copy-done.2
  2.4 0.0 copy-done.1
  2.4 0.0 copy-done.3
  2.4 36.5 %shard_map.64 = bf16[64,32,32]{2,1,0:T(8,128)(2,1)S(1)} custom-call(bf16[1,2,143,2048]{3,2,1,0:T(8,128)(2,1)S(1)} %copy.7.volt_hbm, f32[1,128]{1,0:T(1,128)S(1)} %copy-done.3, s32[1]{0:T(128)S(6)} %copy.9.row_ref, f32[16,16,128]{2,1,0:T(8,128)S(1)} %copy-done.1, f32[2,16,128]{2,1,0:T(8,128)S(1)} %copy-done.2, bf16[256,256]{1,0:T(8,128)(2,1)S(1)} %copy-done), custom_call_target="tpu_custom_call" | custom-call | tf_op jit(solution)/shard_map/pallas_call | solution.py:420
  38.9 1.3 %copy.8 = bf16[64,32,32]{0,2,1:T(8,128)(2,1)} copy(bf16[64,32,32]{2,1,0:T(8,128)(2,1)S(1)} %shard_map.64) | data formatting | bytes 262144 | tf_op jit(solution)/shard_map/pallas_call | solution.py:420
Async XLA Ops:
  0.0 2.4 %copy-start = (bf16[256,256]{1,0:T(8,128)(2,1)S(1)}, bf16[256,256]{1,0:T(8,128)(2,1)}, u32[]{:S(2)}) copy-start(bf16[256,256]{1,0:T(8,128)(2,1)} %constant.12.matrix_ref) | copy-start | bytes 393220
  0.0 2.4 %copy-start.2 = (f32[2,16,128]{2,1,0:T(8,128)S(1)}, f32[2,16,128]{2,1,0:T(8,128)}, u32[]{:S(2)}) copy-start(f32[2,16,128]{2,1,0:T(8,128)} %constant.7.clone.twist_ref) | copy-start | bytes 49156
  0.0 2.4 %copy-start.1 = (f32[16,16,128]{2,1,0:T(8,128)S(1)}, f32[16,16,128]{2,1,0:T(8,128)}, u32[]{:S(2)}) copy-start(f32[16,16,128]{2,1,0:T(8,128)} %constant.6.clone.taper_ref) | copy-start | bytes 393220
  0.0 2.4 %copy-start.3 = (f32[1,128]{1,0:T(1,128)S(1)}, f32[1,128]{1,0:T(1,128)}, u32[]{:S(2)}) copy-start(f32[1,128]{1,0:T(1,128)} %flags_ref.1) | copy-start | bytes 1540

commit v3 on v2

--- a/solution.py
+++ b/solution.py
@@ -208,12 +208,12 @@
 def kernel(
     stn_count, chan_count, chunks,
     volt_hbm, flags_ref, row_ref, taper_ref, twist_ref, matrix_ref, out_ref,
-    volt, wide, filt, mids, send, recv, meta, gathered, acc,
+    volt, wide, filt, mids, send, recv, meta, gathered, masks, acc,
     load_sem, send_sem, recv_sem, meta_send_sem, meta_recv_sem,
 ):
     devices = stn_count * chan_count
     outer, taps = taper_ref.shape[0], taper_ref.shape[1]
-    frames = volt.shape[1]
+    frames = volt.shape[0]
     spectra = flags_ref.shape[1]
     span = spectra // chunks
     packed = LANES // span
@@ -273,19 +273,20 @@
 
         def widen(a, carry, low=low, high=high):
             lanes = pl.ds(pl.multiple_of(a * LANES, LANES), LANES)
-            for part in range(2):
-                wide[part, a, low:high, :] = volt[part, low:high, lanes].astype(jnp.float32)
+            pairs = volt[low:high, :, lanes].reshape(2 * (high - low), LANES)
+            wide[a, 2 * low : 2 * high, :] = pairs.astype(jnp.float32)
             return carry
 
         lax.fori_loop(0, outer, widen, 0)
 
         def fir(a, carry, start=start):
             for part in range(2):
-                total = taper_ref[a, 0:1, :] * wide[part, a, start : start + span, :]
+                def window(tap):
+                    return wide[a, pl.ds(2 * (start + tap) + part, span, stride=2), :]
+
+                total = taper_ref[a, 0:1, :] * window(0)
                 for tap in range(1, taps):
-                    total = total + taper_ref[a, tap : tap + 1, :] * wide[
-                        part, a, start + tap : start + tap + span, :
-                    ]
+                    total = total + taper_ref[a, tap : tap + 1, :] * window(tap)
                 filt[part, a] = total
             return carry
 
@@ -362,8 +363,12 @@
     columns = jnp.logical_and(
         place == lane_at % devices, iota((tall, tall), 0) // devices == lane_at // devices
     ).astype(jnp.bfloat16)
-    row_of = (across[:devices, :devices] == iota((devices, devices), 0)).astype(jnp.bfloat16)
+    rows = jnp.logical_and(
+        across == iota((tall, tall), 0) % devices, iota((tall, tall), 0) // devices == lane_at // devices
+    ).astype(jnp.bfloat16)
     lane = iota((devices, 2 * LANES), 1) % LANES // span
+    for j in range(packed):
+        masks[j] = (lane == j).astype(jnp.bfloat16)
     for chunk in range(chunks):
         arrived = recv.at[chunk, pl.ds(0, devices - 1)]
         pltpu.make_async_copy(arrived, arrived, recv_sem.at[chunk]).wait()
@@ -376,10 +381,7 @@
                 plain = jnp.concatenate([re, im], axis=1)
                 turned = jnp.concatenate([im, -re], axis=1)
                 left = jnp.concatenate([plain, turned], axis=0)
-                zero = jnp.zeros_like(plain)
-                right = jnp.concatenate(
-                    [jnp.where(lane == j, plain, zero) for j in range(packed)], axis=0
-                )
+                right = jnp.concatenate([plain * masks[j] for j in range(packed)], axis=0)
                 product = lax.dot_general(
                     left, right, (((1,), (1,)), ((), ())), preferred_element_type=jnp.float32
                 )
@@ -388,15 +390,24 @@
                 else:
                     acc[quad * groups + group] += product
 
-    for g in range(quads * groups):
-        both = acc[g]
-        chosen = jnp.where(lower, both[:devices], both[devices:]) / denom
-        moved = jnp.dot(chosen.astype(jnp.bfloat16), columns, preferred_element_type=jnp.float32)
+    for first in range(0, quads * groups, packed):
+        chosen = [
+            jnp.where(lower, acc[g, :devices], acc[g, devices:]) / denom
+            for g in range(first, first + packed)
+        ]
         moved = jnp.dot(
-            row_of, moved.astype(jnp.bfloat16), preferred_element_type=jnp.float32
+            jnp.concatenate(chosen, axis=0).astype(jnp.bfloat16),
+            columns,
+            preferred_element_type=jnp.float32,
+        )
+        moved = jnp.dot(
+            rows, moved.astype(jnp.bfloat16), preferred_element_type=jnp.float32
         ).astype(jnp.bfloat16)
-        for j in range(packed):
-            out_ref[packed * g + j] = moved[:, devices * j : devices * (j + 1)]
+        for g in range(packed):
+            for j in range(packed):
+                out_ref[packed * (first + g) + j] = moved[
+                    devices * g : devices * (g + 1), devices * j : devices * (j + 1)
+                ]
 
     for chunk in range(chunks):
         gone = send.at[chunk, pl.ds(0, devices - 1)]
@@ -421,7 +432,7 @@
         functools.partial(kernel, stn_count, chan_count, chunks),
         out_shape=jax.ShapeDtypeStruct((lanes // devices, devices, devices), bf16),
         in_specs=[
-            pl.BlockSpec(memory_space=pl.ANY),
+            pl.BlockSpec(memory_space=pltpu.HBM),
             vmem,
             pl.BlockSpec(memory_space=pltpu.SMEM),
             vmem,
@@ -430,14 +441,15 @@
         ],
         out_specs=vmem,
         scratch_shapes=[
-            pltpu.VMEM((2, frames, lanes), bf16),
-            pltpu.VMEM((2, outer, frames, LANES), f32),
+            pltpu.VMEM((frames, 2, lanes), bf16),
+            pltpu.VMEM((outer, 2 * frames, LANES), f32),
             pltpu.VMEM((2, outer, span, LANES), f32),
             pltpu.VMEM((outer, span, 2 * LANES), f32),
             pltpu.VMEM((chunks, devices, block, LANES), bf16),
             pltpu.VMEM((chunks, devices, block, LANES), bf16),
             pltpu.VMEM((stn_count, ROWS, LANES), f32),
             pltpu.VMEM((devices * block, LANES), f32),
+            pltpu.VMEM((packed, devices, 2 * LANES), bf16),
             pltpu.VMEM((outer * (LANES // devices) // packed, 2 * devices, packed * devices), f32),
             pltpu.SemaphoreType.DMA,
             pltpu.SemaphoreType.DMA((chunks,)),
@@ -448,7 +460,7 @@
         compiler_params=pltpu.CompilerParams(
             collective_id=0, has_side_effects=True, vmem_limit_bytes=32 * 1024 * 1024
         ),
-    )(voltages, flags, station_row, taper, twist, matrix)
+    )(jnp.transpose(voltages, (0, 2, 1, 3)), flags, station_row, taper, twist, matrix)
 
 
 def solution(mesh):

time: 40.3 us -> 41.4 us (1.027)
  local copies, waits for them, and re-layouts: 2.97 us -> 5.71 us
  Pallas kernels: 36.5 us -> 34.8 us
    unnamed x9 -> x10, local copies, waits for them, and re-layouts: 1.7 us -> 4.44 us
    pallas_call x1, Pallas kernels: 36.5 us -> 34.8 us  [fused(): pl.pallas_call(functools.partial(kernel, stn_count, chan_count, chunks),...]
where the time goes in v3:
time: 41.4 us; the launch traced here: 41.2 us
  Pallas kernels  34.8 us (84%)
  local copies, waits for them, and re-layouts  5.71 us (14%)
  between operations  0.67 us (2%)
    pallas_call x1, Pallas kernels, fused(): pl.pallas_call(functools.partial(kernel, stn_count, chan_count, chunks),...  34.8 us
    unnamed x10, local copies, waits for them, and re-layouts  4.44 us
    pallas_call x1, local copies, waits for them, and re-layouts, fused(): pl.pallas_call(functools.partial(kernel, stn_count, chan_count, chunks),...  1.27 us

profile of v3, /device:TPU:0, one launch (start us, length us, event | category | flops | bytes accessed | tf_op | source)
XLA Modules:
  0.0 41.2 jit_solution(15358505041340379441)
XLA Ops:
  0.7 0.0 copy-start
  0.7 1.3 %copy-done = bf16[1,2,143,2048]{3,1,2,0:T(2,128)(2,1)S(1)} copy-done((bf16[1,2,143,2048]{3,1,2,0:T(2,128)(2,1)S(1)}, bf16[1,2,143,2048]{3,1,2,0:T(2,128)(2,1)}, u32[]{:S(2)}) %copy-start) | copy-done | bytes 1171480
  1.9 0.0 copy-start.1
  1.9 0.9 %copy-done.1 = bf16[256,256]{1,0:T(8,128)(2,1)S(1)} copy-done((bf16[256,256]{1,0:T(8,128)(2,1)S(1)}, bf16[256,256]{1,0:T(8,128)(2,1)}, u32[]{:S(2)}) %copy-start.1) | copy-done | bytes 131096
  2.8 0.0 copy-start.2
  2.8 0.9 %copy-done.2 = f32[16,16,128]{2,1,0:T(8,128)S(1)} copy-done((f32[16,16,128]{2,1,0:T(8,128)S(1)}, f32[16,16,128]{2,1,0:T(8,128)}, u32[]{:S(2)}) %copy-start.2) | copy-done | bytes 131096
  3.7 0.0 copy-start.3
  3.7 0.7 %copy-done.3 = f32[2,16,128]{2,1,0:T(8,128)S(1)} copy-done((f32[2,16,128]{2,1,0:T(8,128)S(1)}, f32[2,16,128]{2,1,0:T(8,128)}, u32[]{:S(2)}) %copy-start.3) | copy-done | bytes 16408
  4.4 0.0 copy-start.4
  4.5 0.7 %copy-done.4 = f32[1,128]{1,0:T(1,128)S(1)} copy-done((f32[1,128]{1,0:T(1,128)S(1)}, f32[1,128]{1,0:T(1,128)}, u32[]{:S(2)}) %copy-start.4) | copy-done | bytes 536
  5.1 34.8 %shard_map.64 = bf16[64,32,32]{2,1,0:T(8,128)(2,1)S(1)} custom-call(bf16[1,143,2,2048]{3,2,1,0:T(2,128)(2,1)S(1)} %bitcast.1, f32[1,128]{1,0:T(1,128)S(1)} %copy-done.4, s32[1]{0:T(128)S(6)} %copy.8.row_ref, f32[16,16,128]{2,1,0:T(8,128)S(1)} %copy-done.2, f32[2,16,128]{2,1,0:T(8,128)S(1)} %copy-done.3, bf16[256,256]{1,0:T(8,128)(2,1)S(1)} %copy-done.1), custom_call_target="tpu_custom_call" | custom-call | tf_op jit(solution)/shard_map/pallas_call | solution.py:431
  39.9 1.3 %copy.7 = bf16[64,32,32]{0,2,1:T(8,128)(2,1)} copy(bf16[64,32,32]{2,1,0:T(8,128)(2,1)S(1)} %shard_map.64) | data formatting | bytes 262144 | tf_op jit(solution)/shard_map/pallas_call | solution.py:431
Async XLA Ops:
  0.7 1.3 %copy-start = (bf16[1,2,143,2048]{3,1,2,0:T(2,128)(2,1)S(1)}, bf16[1,2,143,2048]{3,1,2,0:T(2,128)(2,1)}, u32[]{:S(2)}) copy-start(bf16[1,2,143,2048]{3,1,2,0:T(2,128)(2,1)} %param.6) | copy-start | bytes 3514372
  1.9 0.9 %copy-start.1 = (bf16[256,256]{1,0:T(8,128)(2,1)S(1)}, bf16[256,256]{1,0:T(8,128)(2,1)}, u32[]{:S(2)}) copy-start(bf16[256,256]{1,0:T(8,128)(2,1)} %constant.12.matrix_ref) | copy-start | bytes 393220
  2.8 0.9 %copy-start.2 = (f32[16,16,128]{2,1,0:T(8,128)S(1)}, f32[16,16,128]{2,1,0:T(8,128)}, u32[]{:S(2)}) copy-start(f32[16,16,128]{2,1,0:T(8,128)} %constant.6.clone.taper_ref) | copy-start | bytes 393220
  3.7 0.7 %copy-start.3 = (f32[2,16,128]{2,1,0:T(8,128)S(1)}, f32[2,16,128]{2,1,0:T(8,128)}, u32[]{:S(2)}) copy-start(f32[2,16,128]{2,1,0:T(8,128)} %constant.7.clone.twist_ref) | copy-start | bytes 49156
  4.4 0.7 %copy-start.4 = (f32[1,128]{1,0:T(1,128)S(1)}, f32[1,128]{1,0:T(1,128)}, u32[]{:S(2)}) copy-start(f32[1,128]{1,0:T(1,128)} %flags_ref.1) | copy-start | bytes 1540

commit v4 on v3

--- a/solution.py
+++ b/solution.py
@@ -159,7 +159,7 @@
     return (
         jnp.asarray(taper.astype(np.float32)),
         jnp.asarray(twist.astype(np.float32)),
-        jnp.asarray(matrix.astype(np.float32)).astype(jnp.bfloat16),
+        jnp.asarray(matrix.astype(jnp.bfloat16).astype(np.float32)),
     )
 
 
@@ -207,8 +207,9 @@
 
 def kernel(
     stn_count, chan_count, chunks,
-    volt_hbm, flags_ref, row_ref, taper_ref, twist_ref, matrix_ref, out_ref,
-    volt, wide, filt, mids, send, recv, meta, gathered, masks, acc,
+    volt_hbm, flags_hbm, row_ref, taper_hbm, twist_hbm, matrix_hbm, out_ref,
+    volt, flags_ref, taper_ref, twist_ref, matrix_f32, matrix_ref,
+    wide, filt, mids, send, recv, meta, gathered, masks, acc,
     load_sem, send_sem, recv_sem, meta_send_sem, meta_recv_sem,
 ):
     devices = stn_count * chan_count
@@ -224,8 +225,22 @@
     me = stn * chan_count + chan
     bits = devices.bit_length() - 1
 
-    load = pltpu.make_async_copy(volt_hbm.at[0], volt, load_sem)
-    load.start()
+    first_frames = spectra // chunks + taps
+    head, rest = pl.ds(0, first_frames), pl.ds(first_frames, frames - first_frames)
+    sources = (
+        (flags_hbm, flags_ref),
+        (volt_hbm.at[0, head], volt.at[head]),
+        (taper_hbm, taper_ref),
+        (twist_hbm, twist_ref),
+        (matrix_hbm, matrix_f32),
+        (volt_hbm.at[0, rest], volt.at[rest]),
+    )
+    loads = [
+        pltpu.make_async_copy(source, target, load_sem.at[k])
+        for k, (source, target) in enumerate(sources)
+    ]
+    for load in loads:
+        load.start()
 
     def partner(step):
         other = jnp.int32(0)
@@ -245,6 +260,7 @@
 
     lax.fori_loop(1, devices, greet, 0)
 
+    loads[0].wait()
     flags8 = jnp.broadcast_to(flags_ref[...], (ROWS, LANES))
     station = jnp.broadcast_to(row_ref[0], (ROWS, LANES)).astype(jnp.float32)
     meta[stn] = jnp.where(iota((ROWS, LANES), 0) == 0, flags8, station)
@@ -264,7 +280,8 @@
             device_id_type=pl.DeviceIdType.MESH,
         )
 
-    load.wait()
+    for load in loads[1:4]:
+        load.wait()
     lane8 = iota((ROWS, LANES), 1)
     for chunk in range(chunks):
         start = chunk * span
@@ -277,6 +294,8 @@
             wide[a, 2 * low : 2 * high, :] = pairs.astype(jnp.float32)
             return carry
 
+        if chunk == 1:
+            loads[5].wait()
         lax.fori_loop(0, outer, widen, 0)
 
         def fir(a, carry, start=start):
@@ -309,6 +328,9 @@
             shift = (span * j - start) % LANES
             rolled = pltpu.roll(flags8, shift, 1) if shift else flags8
             weights8 = jnp.where(lane8 // span == j, rolled, weights8)
+        if chunk == 0:
+            loads[4].wait()
+            matrix_ref[...] = matrix_f32[...].astype(jnp.bfloat16)
         for pair in range(groups // 2):
             halves = []
             for group in (2 * pair, 2 * pair + 1):
@@ -427,21 +449,27 @@
     block = outer // packed * ROWS
     taper, twist, matrix = host_tables(taps, lanes, devices)
     vmem = pl.BlockSpec(memory_space=pltpu.VMEM)
+    hbm = pl.BlockSpec(memory_space=pl.ANY)
     f32, bf16 = jnp.float32, jnp.bfloat16
     return pl.pallas_call(
         functools.partial(kernel, stn_count, chan_count, chunks),
         out_shape=jax.ShapeDtypeStruct((lanes // devices, devices, devices), bf16),
         in_specs=[
-            pl.BlockSpec(memory_space=pltpu.HBM),
-            vmem,
+            hbm,
+            hbm,
             pl.BlockSpec(memory_space=pltpu.SMEM),
-            vmem,
-            vmem,
-            vmem,
+            hbm,
+            hbm,
+            hbm,
         ],
         out_specs=vmem,
         scratch_shapes=[
             pltpu.VMEM((frames, 2, lanes), bf16),
+            pltpu.VMEM(flags.shape, f32),
+            pltpu.VMEM(taper.shape, f32),
+            pltpu.VMEM(twist.shape, f32),
+            pltpu.VMEM(matrix.shape, f32),
+            pltpu.VMEM(matrix.shape, bf16),
             pltpu.VMEM((outer, 2 * frames, LANES), f32),
             pltpu.VMEM((2, outer, span, LANES), f32),
             pltpu.VMEM((outer, span, 2 * LANES), f32),
@@ -451,14 +479,14 @@
             pltpu.VMEM((devices * block, LANES), f32),
             pltpu.VMEM((packed, devices, 2 * LANES), bf16),
             pltpu.VMEM((outer * (LANES // devices) // packed, 2 * devices, packed * devices), f32),
-            pltpu.SemaphoreType.DMA,
+            pltpu.SemaphoreType.DMA((6,)),
             pltpu.SemaphoreType.DMA((chunks,)),
             pltpu.SemaphoreType.DMA((chunks,)),
             pltpu.SemaphoreType.DMA,
             pltpu.SemaphoreType.DMA,
         ],
         compiler_params=pltpu.CompilerParams(
-            collective_id=0, has_side_effects=True, vmem_limit_bytes=32 * 1024 * 1024
+            collective_id=0, has_side_effects=True, vmem_limit_bytes=63 * 1024 * 1024
         ),
     )(jnp.transpose(voltages, (0, 2, 1, 3)), flags, station_row, taper, twist, matrix)
 

time: 41.4 us -> 38.5 us (0.930)
  local copies, waits for them, and re-layouts: 5.71 us -> 2.26 us
  Pallas kernels: 34.8 us -> 35.4 us
    unnamed x10 -> x0, local copies, waits for them, and re-layouts: 4.44 us -> none
    pallas_call x1, local copies, waits for them, and re-layouts: 1.27 us -> 2.26 us  [fused(): pl.pallas_call(functools.partial(kernel, stn_count, chan_count, chunks),...]
    pallas_call x1, Pallas kernels: 34.8 us -> 35.4 us  [fused(): pl.pallas_call(functools.partial(kernel, stn_count, chan_count, chunks),...]
where the time goes in v4:
time: 38.5 us; the launch traced here: 38.4 us
  Pallas kernels  35.4 us (92%)
  local copies, waits for them, and re-layouts  2.26 us (6%)
  between operations  0.66 us (2%)
    pallas_call x1, Pallas kernels, fused(): pl.pallas_call(functools.partial(kernel, stn_count, chan_count, chunks),...  35.4 us
    pallas_call x1, local copies, waits for them, and re-layouts, fused(): pl.pallas_call(functools.partial(kernel, stn_count, chan_count, chunks),...  2.26 us

profile of v4, /device:TPU:0, one launch (start us, length us, event | category | flops | bytes accessed | tf_op | source)
XLA Modules:
  0.0 38.4 jit_solution(14600763445901561754)
XLA Ops:
  0.7 35.4 %shard_map.64 = bf16[64,32,32]{2,1,0:T(8,128)(2,1)} custom-call(bf16[1,143,2,2048]{3,2,1,0:T(2,128)(2,1)} %bitcast.1, f32[1,128]{1,0:T(1,128)} %flags_hbm.1, s32[1]{0:T(128)S(6)} %copy.8.row_ref, f32[16,16,128]{2,1,0:T(8,128)} %constant.6.clone.taper_hbm, f32[2,16,128]{2,1,0:T(8,128)} %constant.7.clone.twist_hbm, f32[256,256]{1,0:T(8,128)} %constant.8.clone.matrix_hbm), custom_call_target="tpu_custom_call" | custom-call | tf_op jit(solution)/shard_map/pallas_call | solution.py:454
  36.1 2.3 %copy.7 = bf16[64,32,32]{0,2,1:T(8,128)(2,1)} copy(bf16[64,32,32]{2,1,0:T(8,128)(2,1)} %shard_map.64) | data formatting | bytes 262144 | tf_op jit(solution)/shard_map/pallas_call | solution.py:454

commit v5 on v4

--- a/solution.py
+++ b/solution.py
@@ -156,11 +156,13 @@
     real_rows = np.concatenate([cos, sin], axis=1).reshape(devices, 1, quads, 2 * LANES)
     imag_rows = np.concatenate([-sin, cos], axis=1).reshape(devices, 1, quads, 2 * LANES)
     matrix = np.concatenate([real_rows, imag_rows], axis=1).reshape(2 * LANES, 2 * LANES)
-    return (
-        jnp.asarray(taper.astype(np.float32)),
-        jnp.asarray(twist.astype(np.float32)),
-        jnp.asarray(matrix.astype(jnp.bfloat16).astype(np.float32)),
-    )
+    rows = [
+        np.repeat(taper.reshape(outer * taps, LANES), ROWS, axis=0),
+        twist.reshape(2 * outer, LANES),
+        matrix.astype(jnp.bfloat16).astype(np.float32)[:, :LANES],
+        matrix.astype(jnp.bfloat16).astype(np.float32)[:, LANES:],
+    ]
+    return jnp.asarray(np.concatenate(rows, axis=0).astype(np.float32))
 
 
 def dft4(a, b, c, d):
@@ -207,15 +209,16 @@
 
 def kernel(
     stn_count, chan_count, chunks,
-    volt_hbm, flags_hbm, row_ref, taper_hbm, twist_hbm, matrix_hbm, out_ref,
-    volt, flags_ref, taper_ref, twist_ref, matrix_f32, matrix_ref,
+    volt_hbm, flags_ref, row_ref, table_hbm, out_ref,
+    volt, taper_ref, twist_ref, matrix_f32, matrix_ref,
     wide, filt, mids, send, recv, meta, gathered, masks, acc,
     load_sem, send_sem, recv_sem, meta_send_sem, meta_recv_sem,
 ):
     devices = stn_count * chan_count
-    outer, taps = taper_ref.shape[0], taper_ref.shape[1]
     frames = volt.shape[0]
     spectra = flags_ref.shape[1]
+    taps = frames - spectra + 1
+    outer = volt.shape[2] // LANES
     span = spectra // chunks
     packed = LANES // span
     groups = outer // packed
@@ -227,12 +230,12 @@
 
     first_frames = spectra // chunks + taps
     head, rest = pl.ds(0, first_frames), pl.ds(first_frames, frames - first_frames)
+    taper_rows, twist_rows, matrix_rows = outer * taps * ROWS, 2 * outer, 4 * LANES
     sources = (
-        (flags_hbm, flags_ref),
         (volt_hbm.at[0, head], volt.at[head]),
-        (taper_hbm, taper_ref),
-        (twist_hbm, twist_ref),
-        (matrix_hbm, matrix_f32),
+        (table_hbm.at[pl.ds(0, taper_rows)], taper_ref),
+        (table_hbm.at[pl.ds(taper_rows, twist_rows)], twist_ref),
+        (table_hbm.at[pl.ds(taper_rows + twist_rows, matrix_rows)], matrix_f32),
         (volt_hbm.at[0, rest], volt.at[rest]),
     )
     loads = [
@@ -260,8 +263,11 @@
 
     lax.fori_loop(1, devices, greet, 0)
 
-    loads[0].wait()
-    flags8 = jnp.broadcast_to(flags_ref[...], (ROWS, LANES))
+    lane8 = iota((ROWS, LANES), 1)
+    flags8 = lax.fori_loop(
+        0, spectra, lambda t, held: jnp.where(lane8 == t, flags_ref[0, t], held),
+        jnp.zeros((ROWS, LANES), jnp.float32), unroll=8,
+    )
     station = jnp.broadcast_to(row_ref[0], (ROWS, LANES)).astype(jnp.float32)
     meta[stn] = jnp.where(iota((ROWS, LANES), 0) == 0, flags8, station)
 
@@ -280,9 +286,8 @@
             device_id_type=pl.DeviceIdType.MESH,
         )
 
-    for load in loads[1:4]:
+    for load in loads[:3]:
         load.wait()
-    lane8 = iota((ROWS, LANES), 1)
     for chunk in range(chunks):
         start = chunk * span
         low = 0 if chunk == 0 else start + taps
@@ -295,18 +300,23 @@
             return carry
 
         if chunk == 1:
-            loads[5].wait()
+            loads[4].wait()
         lax.fori_loop(0, outer, widen, 0)
 
         def fir(a, carry, start=start):
             for part in range(2):
                 def window(tap):
-                    return wide[a, pl.ds(2 * (start + tap) + part, span, stride=2), :]
-
-                total = taper_ref[a, 0:1, :] * window(0)
+                    rows = wide[a, pl.ds(2 * (start + tap) + part, span, stride=2), :]
+                    return rows.reshape(span // ROWS, ROWS, LANES)
+
+                def weight(tap):
+                    at = pl.multiple_of((a * taps + tap) * ROWS, ROWS)
+                    return taper_ref[pl.ds(at, ROWS), :][None]
+
+                total = weight(0) * window(0)
                 for tap in range(1, taps):
-                    total = total + taper_ref[a, tap : tap + 1, :] * window(tap)
-                filt[part, a] = total
+                    total = total + weight(tap) * window(tap)
+                filt[part, a] = total.reshape(span, LANES)
             return carry
 
         lax.fori_loop(0, outer, fir, 0)
@@ -316,7 +326,8 @@
             values = dft16([(filt[0, a, rows, :], filt[1, a, rows, :]) for a in range(outer)])
             for k in range(outer):
                 re, im = values[k]
-                c, s = twist_ref[0, k : k + 1, :], twist_ref[1, k : k + 1, :]
+                c = twist_ref[k : k + 1, :]
+                s = twist_ref[outer + k : outer + k + 1, :]
                 mids[k, rows, 0:LANES] = re * c + im * s
                 mids[k, rows, LANES:] = im * c - re * s
             return carry
@@ -329,8 +340,12 @@
             rolled = pltpu.roll(flags8, shift, 1) if shift else flags8
             weights8 = jnp.where(lane8 // span == j, rolled, weights8)
         if chunk == 0:
-            loads[4].wait()
-            matrix_ref[...] = matrix_f32[...].astype(jnp.bfloat16)
+            loads[3].wait()
+            for half in range(2):
+                columns = slice(half * LANES, (half + 1) * LANES)
+                matrix_ref[:, columns] = matrix_f32[
+                    2 * LANES * half : 2 * LANES * (half + 1)
+                ].astype(jnp.bfloat16)
         for pair in range(groups // 2):
             halves = []
             for group in (2 * pair, 2 * pair + 1):
@@ -447,7 +462,7 @@
     span = spectra // chunks
     packed = LANES // span
     block = outer // packed * ROWS
-    taper, twist, matrix = host_tables(taps, lanes, devices)
+    table = host_tables(taps, lanes, devices)
     vmem = pl.BlockSpec(memory_space=pltpu.VMEM)
     hbm = pl.BlockSpec(memory_space=pl.ANY)
     f32, bf16 = jnp.float32, jnp.bfloat16
@@ -456,20 +471,17 @@
         out_shape=jax.ShapeDtypeStruct((lanes // devices, devices, devices), bf16),
         in_specs=[
             hbm,
-            hbm,
             pl.BlockSpec(memory_space=pltpu.SMEM),
-            hbm,
-            hbm,
+            pl.BlockSpec(memory_space=pltpu.SMEM),
             hbm,
         ],
         out_specs=vmem,
         scratch_shapes=[
             pltpu.VMEM((frames, 2, lanes), bf16),
-            pltpu.VMEM(flags.shape, f32),
-            pltpu.VMEM(taper.shape, f32),
-            pltpu.VMEM(twist.shape, f32),
-            pltpu.VMEM(matrix.shape, f32),
-            pltpu.VMEM(matrix.shape, bf16),
+            pltpu.VMEM((outer * taps * ROWS, LANES), f32),
+            pltpu.VMEM((2 * outer, LANES), f32),
+            pltpu.VMEM((4 * LANES, LANES), f32),
+            pltpu.VMEM((2 * LANES, 2 * LANES), bf16),
             pltpu.VMEM((outer, 2 * frames, LANES), f32),
             pltpu.VMEM((2, outer, span, LANES), f32),
             pltpu.VMEM((outer, span, 2 * LANES), f32),
@@ -479,16 +491,16 @@
             pltpu.VMEM((devices * block, LANES), f32),
             pltpu.VMEM((packed, devices, 2 * LANES), bf16),
             pltpu.VMEM((outer * (LANES // devices) // packed, 2 * devices, packed * devices), f32),
-            pltpu.SemaphoreType.DMA((6,)),
+            pltpu.SemaphoreType.DMA((5,)),
             pltpu.SemaphoreType.DMA((chunks,)),
             pltpu.SemaphoreType.DMA((chunks,)),
             pltpu.SemaphoreType.DMA,
             pltpu.SemaphoreType.DMA,
         ],
         compiler_params=pltpu.CompilerParams(
-            collective_id=0, has_side_effects=True, vmem_limit_bytes=63 * 1024 * 1024
+            collective_id=0, has_side_effects=True, vmem_limit_bytes=53 * 1024 * 1024
         ),
-    )(jnp.transpose(voltages, (0, 2, 1, 3)), flags, station_row, taper, twist, matrix)
+    )(jnp.transpose(voltages, (0, 2, 1, 3)), flags, station_row, table)
 
 
 def solution(mesh):

time: 38.5 us -> 38.1 us (0.990)
    pallas_call x1, local copies, waits for them, and re-layouts: 2.26 us -> 1.27 us  [fused(): pl.pallas_call(functools.partial(kernel, stn_count, chan_count, chunks),...]
    unnamed x0 -> x2, local copies, waits for them, and re-layouts: none -> 0.65 us
where the time goes in v5:
time: 38.1 us; the launch traced here: 38 us
  Pallas kernels  35.4 us (93%)
  local copies, waits for them, and re-layouts  1.92 us (5%)
  between operations  0.67 us (2%)
    pallas_call x1, Pallas kernels, fused(): pl.pallas_call(functools.partial(kernel, stn_count, chan_count, chunks),...  35.4 us
    pallas_call x1, local copies, waits for them, and re-layouts, fused(): pl.pallas_call(functools.partial(kernel, stn_count, chan_count, chunks),...  1.27 us

profile of v5, /device:TPU:0, one launch (start us, length us, event | category | flops | bytes accessed | tf_op | source)
XLA Modules:
  0.0 38.0 jit_solution(17424722625370219430)
XLA Ops:
  0.7 0.0 copy-start
  0.7 0.6 %copy-done = f32[1,128]{1,0:T(1,128)S(1)} copy-done((f32[1,128]{1,0:T(1,128)S(1)}, f32[1,128]{1,0:T(1,128)}, u32[]{:S(2)}) %copy-start) | copy-done | bytes 536
  1.3 35.4 %shard_map.46 = bf16[64,32,32]{2,1,0:T(8,128)(2,1)S(1)} custom-call(bf16[1,143,2,2048]{3,2,1,0:T(2,128)(2,1)} %bitcast.1, f32[1,128]{1,0:T(1,128)S(1)} %copy-done, s32[1]{0:T(128)S(6)} %copy.6.row_ref, f32[2592,128]{1,0:T(8,128)} %constant.2.clone.table_hbm), custom_call_target="tpu_custom_call" | custom-call | tf_op jit(solution)/shard_map/pallas_call | solution.py:469
  36.7 1.3 %copy.5 = bf16[64,32,32]{0,2,1:T(8,128)(2,1)} copy(bf16[64,32,32]{2,1,0:T(8,128)(2,1)S(1)} %shard_map.46) | data formatting | bytes 262144 | tf_op jit(solution)/shard_map/pallas_call | solution.py:469
Async XLA Ops:
  0.7 0.7 %copy-start = (f32[1,128]{1,0:T(1,128)S(1)}, f32[1,128]{1,0:T(1,128)}, u32[]{:S(2)}) copy-start(f32[1,128]{1,0:T(1,128)} %flags_ref.1) | copy-start | bytes 1540

commit v6 on v5

--- a/solution.py
+++ b/solution.py
@@ -226,7 +226,6 @@
     block = groups * ROWS
     stn, chan = lax.axis_index("stn"), lax.axis_index("chan")
     me = stn * chan_count + chan
-    bits = devices.bit_length() - 1
 
     first_frames = spectra // chunks + taps
     head, rest = pl.ds(0, first_frames), pl.ds(first_frames, frames - first_frames)
@@ -245,23 +244,30 @@
     for load in loads:
         load.start()
 
+    stn_flips = [
+        (1 - 2 * (stn // 2**bit % 2)) * 2**bit for bit in range(stn_count.bit_length() - 1)
+    ]
+    chan_flips = [
+        (1 - 2 * (chan // 2**bit % 2)) * 2**bit for bit in range(chan_count.bit_length() - 1)
+    ]
+
+    def flipped(start, flips, step):
+        for bit, flip in enumerate(flips):
+            if step >> bit & 1:
+                start = start + flip
+        return start
+
     def partner(step):
-        other = jnp.int32(0)
-        for bit in range(bits):
-            other = other + ((me // 2**bit + step // 2**bit) % 2) * 2**bit
-        return other
+        return (
+            flipped(stn, stn_flips, step // chan_count),
+            flipped(chan, chan_flips, step % chan_count),
+        )
 
     barrier = pltpu.get_barrier_semaphore()
-
-    def greet(step, carry):
-        other = partner(step)
+    for step in range(1, devices):
         pl.semaphore_signal(
-            barrier, inc=1, device_id=(other // chan_count, other % chan_count),
-            device_id_type=pl.DeviceIdType.MESH,
+            barrier, inc=1, device_id=partner(step), device_id_type=pl.DeviceIdType.MESH
         )
-        return carry
-
-    lax.fori_loop(1, devices, greet, 0)
 
     lane8 = iota((ROWS, LANES), 1)
     flags8 = lax.fori_loop(
@@ -271,19 +277,19 @@
     station = jnp.broadcast_to(row_ref[0], (ROWS, LANES)).astype(jnp.float32)
     meta[stn] = jnp.where(iota((ROWS, LANES), 0) == 0, flags8, station)
 
-    def meta_copy(other):
+    def meta_copy(step):
         return pltpu.make_async_remote_copy(
             src_ref=meta.at[stn], dst_ref=meta.at[stn],
             send_sem=meta_send_sem, recv_sem=meta_recv_sem,
-            device_id=(other, chan), device_id_type=pl.DeviceIdType.MESH,
+            device_id=(flipped(stn, stn_flips, step), chan), device_id_type=pl.DeviceIdType.MESH,
         )
 
-    def block_copy(chunk, other):
+    def block_copy(chunk, step):
+        to_stn, to_chan = partner(step)
         return pltpu.make_async_remote_copy(
-            src_ref=send.at[chunk, other], dst_ref=recv.at[chunk, me],
+            src_ref=send.at[chunk, to_stn * chan_count + to_chan], dst_ref=recv.at[chunk, me],
             send_sem=send_sem.at[chunk], recv_sem=recv_sem.at[chunk],
-            device_id=(other // chan_count, other % chan_count),
-            device_id_type=pl.DeviceIdType.MESH,
+            device_id=(to_stn, to_chan), device_id_type=pl.DeviceIdType.MESH,
         )
 
     for load in loads[:3]:
@@ -362,20 +368,14 @@
 
         if chunk == 0:
             pl.semaphore_wait(barrier, devices - 1)
-
-            def tell(step, carry):
-                meta_copy((stn + step) % stn_count).start()
-                return carry
-
-        def push(step, carry, chunk=chunk):
-            far = devices - 1 - (step - 1) // 2
-            near = devices // 2 - step // 2
-            block_copy(chunk, partner(step % 2 * far + (1 - step % 2) * near)).start()
-            return carry
-
-        lax.fori_loop(1, devices, push, 0)
+        half = devices // 2
+        for far in range(devices - 1, half - 1, -1):
+            block_copy(chunk, far).start()
+            if far > half:
+                block_copy(chunk, far - half).start()
         if chunk == 0:
-            lax.fori_loop(1, stn_count, tell, 0)
+            for step in range(1, stn_count):
+                meta_copy(step).start()
         recv[chunk, me] = send[chunk, me]
 
     told = meta.at[pl.ds(0, stn_count - 1)]

time: 38.1 us -> 37.3 us (0.979)
  Pallas kernels: 35.4 us -> 34.6 us
    pallas_call x1, Pallas kernels: 35.4 us -> 34.6 us  [fused(): pl.pallas_call(functools.partial(kernel, stn_count, chan_count, chunks),...]
where the time goes in v6:
time: 37.3 us; the launch traced here: 37.1 us
  Pallas kernels  34.6 us (93%)
  local copies, waits for them, and re-layouts  1.92 us (5%)
  between operations  0.67 us (2%)
    pallas_call x1, Pallas kernels, fused(): pl.pallas_call(functools.partial(kernel, stn_count, chan_count, chunks),...  34.6 us
    pallas_call x1, local copies, waits for them, and re-layouts, fused(): pl.pallas_call(functools.partial(kernel, stn_count, chan_count, chunks),...  1.27 us

profile of v6, /device:TPU:0, one launch (start us, length us, event | category | flops | bytes accessed | tf_op | source)
XLA Modules:
  0.0 37.1 jit_solution(641168477935924043)
XLA Ops:
  0.7 0.0 copy-start
  0.7 0.6 %copy-done = f32[1,128]{1,0:T(1,128)S(1)} copy-done((f32[1,128]{1,0:T(1,128)S(1)}, f32[1,128]{1,0:T(1,128)}, u32[]{:S(2)}) %copy-start) | copy-done | bytes 536
  1.3 34.6 %shard_map.46 = bf16[64,32,32]{2,1,0:T(8,128)(2,1)S(1)} custom-call(bf16[1,143,2,2048]{3,2,1,0:T(2,128)(2,1)} %bitcast.1, f32[1,128]{1,0:T(1,128)S(1)} %copy-done, s32[1]{0:T(128)S(6)} %copy.6.row_ref, f32[2592,128]{1,0:T(8,128)} %constant.2.clone.table_hbm), custom_call_target="tpu_custom_call" | custom-call | tf_op jit(solution)/shard_map/pallas_call | solution.py:469
  35.9 1.3 %copy.5 = bf16[64,32,32]{0,2,1:T(8,128)(2,1)} copy(bf16[64,32,32]{2,1,0:T(8,128)(2,1)S(1)} %shard_map.46) | data formatting | bytes 262144 | tf_op jit(solution)/shard_map/pallas_call | solution.py:469
Async XLA Ops:
  0.7 0.7 %copy-start = (f32[1,128]{1,0:T(1,128)S(1)}, f32[1,128]{1,0:T(1,128)}, u32[]{:S(2)}) copy-start(f32[1,128]{1,0:T(1,128)} %flags_ref.1) | copy-start | bytes 1540

commit v7 on v6

--- a/solution.py
+++ b/solution.py
@@ -394,6 +394,7 @@
     place = 2 * exact(spread, all_rows, (((1,), (0,)), ((), ()))).astype(jnp.int32)
     place = place + iota(place.shape, 0) % 2
     across = place.T
+    place = place[:, :tall]
     lower = place[:devices] >= across[:devices]
     denom = jnp.maximum(count, 1.0)
     lane_at = iota((tall, tall), 1)
@@ -401,7 +402,7 @@
         place == lane_at % devices, iota((tall, tall), 0) // devices == lane_at // devices
     ).astype(jnp.bfloat16)
     rows = jnp.logical_and(
-        across == iota((tall, tall), 0) % devices, iota((tall, tall), 0) // devices == lane_at // devices
+        across[:tall] == iota((tall, tall), 0) % devices, iota((tall, tall), 0) // devices == lane_at // devices
     ).astype(jnp.bfloat16)
     lane = iota((devices, 2 * LANES), 1) % LANES // span
     for j in range(packed):
@@ -458,7 +459,7 @@
     spectra = flags.shape[1]
     taps = frames - spectra + 1
     outer = lanes // LANES
-    chunks = 4
+    chunks = 2
     span = spectra // chunks
     packed = LANES // span
     block = outer // packed * ROWS

time: 37.3 us -> 37.9 us (1.016)
  Pallas kernels: 34.6 us -> 35.2 us
    pallas_call x1, Pallas kernels: 34.6 us -> 35.2 us  [fused(): pl.pallas_call(functools.partial(kernel, stn_count, chan_count, chunks),...]
where the time goes in v7:
time: 37.9 us; the launch traced here: 37.8 us
  Pallas kernels  35.2 us (93%)
  local copies, waits for them, and re-layouts  1.92 us (5%)
  between operations  0.67 us (2%)
    pallas_call x1, Pallas kernels, fused(): pl.pallas_call(functools.partial(kernel, stn_count, chan_count, chunks),...  35.2 us
    pallas_call x1, local copies, waits for them, and re-layouts, fused(): pl.pallas_call(functools.partial(kernel, stn_count, chan_count, chunks),...  1.27 us

profile of v7, /device:TPU:0, one launch (start us, length us, event | category | flops | bytes accessed | tf_op | source)
XLA Modules:
  0.0 37.8 jit_solution(17302761964299029795)
XLA Ops:
  0.7 0.0 copy-start
  0.7 0.6 %copy-done = f32[1,128]{1,0:T(1,128)S(1)} copy-done((f32[1,128]{1,0:T(1,128)S(1)}, f32[1,128]{1,0:T(1,128)}, u32[]{:S(2)}) %copy-start) | copy-done | bytes 536
  1.3 35.2 %shard_map.46 = bf16[64,32,32]{2,1,0:T(8,128)(2,1)S(1)} custom-call(bf16[1,143,2,2048]{3,2,1,0:T(2,128)(2,1)} %bitcast.1, f32[1,128]{1,0:T(1,128)S(1)} %copy-done, s32[1]{0:T(128)S(6)} %copy.6.row_ref, f32[2592,128]{1,0:T(8,128)} %constant.2.clone.table_hbm), custom_call_target="tpu_custom_call" | custom-call | tf_op jit(solution)/shard_map/pallas_call | solution.py:470
  36.5 1.3 %copy.5 = bf16[64,32,32]{0,2,1:T(8,128)(2,1)} copy(bf16[64,32,32]{2,1,0:T(8,128)(2,1)S(1)} %shard_map.46) | data formatting | bytes 262144 | tf_op jit(solution)/shard_map/pallas_call | solution.py:470
Async XLA Ops:
  0.7 0.7 %copy-start = (f32[1,128]{1,0:T(1,128)S(1)}, f32[1,128]{1,0:T(1,128)}, u32[]{:S(2)}) copy-start(f32[1,128]{1,0:T(1,128)} %flags_ref.1) | copy-start | bytes 1540

commit v8 on v6

--- a/solution.py
+++ b/solution.py
@@ -284,10 +284,13 @@
             device_id=(flipped(stn, stn_flips, step), chan), device_id_type=pl.DeviceIdType.MESH,
         )
 
+    trips = {0: (0, 1), chunks - 2: (1, chunks - 2), chunks - 1: (chunks - 1, 1)}
+
     def block_copy(chunk, step):
         to_stn, to_chan = partner(step)
+        batch = pl.ds(*trips[chunk])
         return pltpu.make_async_remote_copy(
-            src_ref=send.at[chunk, to_stn * chan_count + to_chan], dst_ref=recv.at[chunk, me],
+            src_ref=send.at[to_stn * chan_count + to_chan, batch], dst_ref=recv.at[me, batch],
             send_sem=send_sem.at[chunk], recv_sem=recv_sem.at[chunk],
             device_id=(to_stn, to_chan), device_id_type=pl.DeviceIdType.MESH,
         )
@@ -362,12 +365,15 @@
                 )
                 rounded = spectrum.astype(jnp.bfloat16).astype(jnp.float32)
                 halves.append(rounded.reshape(devices, ROWS, LANES) * weights8[None])
-            send[chunk, :, 2 * ROWS * pair : 2 * ROWS * (pair + 1), :] = jnp.concatenate(
+            send[:, chunk, 2 * ROWS * pair : 2 * ROWS * (pair + 1), :] = jnp.concatenate(
                 halves, axis=1
             ).astype(jnp.bfloat16)
 
         if chunk == 0:
             pl.semaphore_wait(barrier, devices - 1)
+        recv[me, chunk] = send[me, chunk]
+        if chunk not in trips:
+            continue
         half = devices // 2
         for far in range(devices - 1, half - 1, -1):
             block_copy(chunk, far).start()
@@ -376,7 +382,6 @@
         if chunk == 0:
             for step in range(1, stn_count):
                 meta_copy(step).start()
-        recv[chunk, me] = send[chunk, me]
 
     told = meta.at[pl.ds(0, stn_count - 1)]
     pltpu.make_async_copy(told, told, meta_recv_sem).wait()
@@ -407,14 +412,18 @@
     for j in range(packed):
         masks[j] = (lane == j).astype(jnp.bfloat16)
     for chunk in range(chunks):
-        arrived = recv.at[chunk, pl.ds(0, devices - 1)]
-        pltpu.make_async_copy(arrived, arrived, recv_sem.at[chunk]).wait()
-        gathered[...] = recv[chunk].reshape(devices * block, LANES).astype(jnp.float32)
+        for last, (low, size) in trips.items():
+            if low == chunk:
+                arrived = recv.at[pl.ds(0, devices - 1), pl.ds(low, size)]
+                pltpu.make_async_copy(arrived, arrived, recv_sem.at[last]).wait()
+        for source in range(devices):
+            at = source * (block + 1)
+            gathered[at : at + block, :] = recv[source, chunk].astype(jnp.float32)
         for quad in range(quads):
             for group in range(groups):
                 at = group * ROWS + quad
-                re = gathered[pl.ds(at, devices, stride=block), :].astype(jnp.bfloat16)
-                im = gathered[pl.ds(at + quads, devices, stride=block), :].astype(jnp.bfloat16)
+                re = gathered[pl.ds(at, devices, stride=block + 1), :].astype(jnp.bfloat16)
+                im = gathered[pl.ds(at + quads, devices, stride=block + 1), :].astype(jnp.bfloat16)
                 plain = jnp.concatenate([re, im], axis=1)
                 turned = jnp.concatenate([im, -re], axis=1)
                 left = jnp.concatenate([plain, turned], axis=0)
@@ -446,9 +455,9 @@
                     devices * g : devices * (g + 1), devices * j : devices * (j + 1)
                 ]
 
-    for chunk in range(chunks):
-        gone = send.at[chunk, pl.ds(0, devices - 1)]
-        pltpu.make_async_copy(gone, gone, send_sem.at[chunk]).wait()
+    for last, (low, size) in trips.items():
+        gone = send.at[pl.ds(0, devices - 1), pl.ds(low, size)]
+        pltpu.make_async_copy(gone, gone, send_sem.at[last]).wait()
     pltpu.make_async_copy(told, told, meta_send_sem).wait()
 
 
@@ -485,10 +494,10 @@
             pltpu.VMEM((outer, 2 * frames, LANES), f32),
             pltpu.VMEM((2, outer, span, LANES), f32),
             pltpu.VMEM((outer, span, 2 * LANES), f32),
-            pltpu.VMEM((chunks, devices, block, LANES), bf16),
-            pltpu.VMEM((chunks, devices, block, LANES), bf16),
+            pltpu.VMEM((devices, chunks, block, LANES), bf16),
+            pltpu.VMEM((devices, chunks, block, LANES), bf16),
             pltpu.VMEM((stn_count, ROWS, LANES), f32),
-            pltpu.VMEM((devices * block, LANES), f32),
+            pltpu.VMEM((devices * (block + 1), LANES), f32),
             pltpu.VMEM((packed, devices, 2 * LANES), bf16),
             pltpu.VMEM((outer * (LANES // devices) // packed, 2 * devices, packed * devices), f32),
             pltpu.SemaphoreType.DMA((5,)),

time: 37.3 us -> 37.3 us (level)
  no operation moved by 1% of the time
where the time goes in v8:
time: 37.3 us; the launch traced here: 37.2 us
  Pallas kernels  34.6 us (93%)
  local copies, waits for them, and re-layouts  1.92 us (5%)
  between operations  0.67 us (2%)
    pallas_call x1, Pallas kernels, fused(): pl.pallas_call(functools.partial(kernel, stn_count, chan_count, chunks),...  34.6 us
    pallas_call x1, local copies, waits for them, and re-layouts, fused(): pl.pallas_call(functools.partial(kernel, stn_count, chan_count, chunks),...  1.27 us

profile of v8, /device:TPU:0, one launch (start us, length us, event | category | flops | bytes accessed | tf_op | source)
XLA Modules:
  0.0 37.2 jit_solution(14934527122352892743)
XLA Ops:
  0.7 0.0 copy-start
  0.7 0.6 %copy-done = f32[1,128]{1,0:T(1,128)S(1)} copy-done((f32[1,128]{1,0:T(1,128)S(1)}, f32[1,128]{1,0:T(1,128)}, u32[]{:S(2)}) %copy-start) | copy-done | bytes 536
  1.3 34.6 %shard_map.46 = bf16[64,32,32]{2,1,0:T(8,128)(2,1)S(1)} custom-call(bf16[1,143,2,2048]{3,2,1,0:T(2,128)(2,1)} %bitcast.1, f32[1,128]{1,0:T(1,128)S(1)} %copy-done, s32[1]{0:T(128)S(6)} %copy.6.row_ref, f32[2592,128]{1,0:T(8,128)} %constant.2.clone.table_hbm), custom_call_target="tpu_custom_call" | custom-call | tf_op jit(solution)/shard_map/pallas_call | solution.py:478
  35.9 1.3 %copy.5 = bf16[64,32,32]{0,2,1:T(8,128)(2,1)} copy(bf16[64,32,32]{2,1,0:T(8,128)(2,1)S(1)} %shard_map.46) | data formatting | bytes 262144 | tf_op jit(solution)/shard_map/pallas_call | solution.py:478
Async XLA Ops:
  0.7 0.7 %copy-start = (f32[1,128]{1,0:T(1,128)S(1)}, f32[1,128]{1,0:T(1,128)}, u32[]{:S(2)}) copy-start(f32[1,128]{1,0:T(1,128)} %flags_ref.1) | copy-start | bytes 1540

commit v9 on v6

--- a/solution.py
+++ b/solution.py
@@ -307,7 +307,7 @@
 
         if chunk == 1:
             loads[4].wait()
-        lax.fori_loop(0, outer, widen, 0)
+        lax.fori_loop(0, outer, widen, 0, unroll=4)
 
         def fir(a, carry, start=start):
             for part in range(2):
@@ -325,7 +325,7 @@
                 filt[part, a] = total.reshape(span, LANES)
             return carry
 
-        lax.fori_loop(0, outer, fir, 0)
+        lax.fori_loop(0, outer, fir, 0, unroll=2)
 
         def first_stage(tile, carry):
             rows = pl.ds(pl.multiple_of(tile * ROWS, ROWS), ROWS)
@@ -338,7 +338,7 @@
                 mids[k, rows, LANES:] = im * c - re * s
             return carry
 
-        lax.fori_loop(0, span // ROWS, first_stage, 0)
+        lax.fori_loop(0, span // ROWS, first_stage, 0, unroll=2)
 
         weights8 = jnp.zeros((ROWS, LANES), jnp.float32)
         for j in range(packed):

time: 37.3 us -> 37.1 us (level)
  no operation moved by 1% of the time
where the time goes in v9:
time: 37.1 us; the launch traced here: 36.9 us
  Pallas kernels  34.4 us (93%)
  local copies, waits for them, and re-layouts  1.92 us (5%)
  between operations  0.67 us (2%)
    pallas_call x1, Pallas kernels, fused(): pl.pallas_call(functools.partial(kernel, stn_count, chan_count, chunks),...  34.4 us
    pallas_call x1, local copies, waits for them, and re-layouts, fused(): pl.pallas_call(functools.partial(kernel, stn_count, chan_count, chunks),...  1.27 us

profile of v9, /device:TPU:0, one launch (start us, length us, event | category | flops | bytes accessed | tf_op | source)
XLA Modules:
  0.0 36.9 jit_solution(10536467473778825732)
XLA Ops:
  0.7 0.0 copy-start
  0.7 0.6 %copy-done = f32[1,128]{1,0:T(1,128)S(1)} copy-done((f32[1,128]{1,0:T(1,128)S(1)}, f32[1,128]{1,0:T(1,128)}, u32[]{:S(2)}) %copy-start) | copy-done | bytes 536
  1.3 34.4 %shard_map.46 = bf16[64,32,32]{2,1,0:T(8,128)(2,1)S(1)} custom-call(bf16[1,143,2,2048]{3,2,1,0:T(2,128)(2,1)} %bitcast.1, f32[1,128]{1,0:T(1,128)S(1)} %copy-done, s32[1]{0:T(128)S(6)} %copy.6.row_ref, f32[2592,128]{1,0:T(8,128)} %constant.2.clone.table_hbm), custom_call_target="tpu_custom_call" | custom-call | tf_op jit(solution)/shard_map/pallas_call | solution.py:469
  35.7 1.3 %copy.5 = bf16[64,32,32]{0,2,1:T(8,128)(2,1)} copy(bf16[64,32,32]{2,1,0:T(8,128)(2,1)S(1)} %shard_map.46) | data formatting | bytes 262144 | tf_op jit(solution)/shard_map/pallas_call | solution.py:469
Async XLA Ops:
  0.7 0.7 %copy-start = (f32[1,128]{1,0:T(1,128)S(1)}, f32[1,128]{1,0:T(1,128)}, u32[]{:S(2)}) copy-start(f32[1,128]{1,0:T(1,128)} %flags_ref.1) | copy-start | bytes 1540

commit v10 on v6

--- a/solution.py
+++ b/solution.py
@@ -284,8 +284,13 @@
             device_id=(flipped(stn, stn_flips, step), chan), device_id_type=pl.DeviceIdType.MESH,
         )
 
-    def block_copy(chunk, step):
-        to_stn, to_chan = partner(step)
+    inner = (stn // (stn_count // 2) + stn // (stn_count // 4)) % 2
+
+    def block_copy(chunk, step, inner_step):
+        to_stn, to_chan = (
+            there + inner * (other - there)
+            for there, other in zip(partner(step), partner(inner_step))
+        )
         return pltpu.make_async_remote_copy(
             src_ref=send.at[chunk, to_stn * chan_count + to_chan], dst_ref=recv.at[chunk, me],
             send_sem=send_sem.at[chunk], recv_sem=recv_sem.at[chunk],
@@ -369,10 +374,10 @@
         if chunk == 0:
             pl.semaphore_wait(barrier, devices - 1)
         half = devices // 2
-        for far in range(devices - 1, half - 1, -1):
-            block_copy(chunk, far).start()
-            if far > half:
-                block_copy(chunk, far - half).start()
+        outer_order = range(devices - 1, 0, -1)
+        inner_order = (*range(half - 1, 0, -1), *range(devices - 1, half - 1, -1))
+        for step, inner_step in zip(outer_order, inner_order):
+            block_copy(chunk, step, inner_step).start()
         if chunk == 0:
             for step in range(1, stn_count):
                 meta_copy(step).start()

time: 37.3 us -> 37.4 us (level)
  no operation moved by 1% of the time
where the time goes in v10:
time: 37.4 us; the launch traced here: 37.2 us
  Pallas kernels  34.6 us (93%)
  local copies, waits for them, and re-layouts  1.92 us (5%)
  between operations  0.67 us (2%)
    pallas_call x1, Pallas kernels, fused(): pl.pallas_call(functools.partial(kernel, stn_count, chan_count, chunks),...  34.6 us
    pallas_call x1, local copies, waits for them, and re-layouts, fused(): pl.pallas_call(functools.partial(kernel, stn_count, chan_count, chunks),...  1.27 us

profile of v10, /device:TPU:0, one launch (start us, length us, event | category | flops | bytes accessed | tf_op | source)
XLA Modules:
  0.0 37.2 jit_solution(2207345880569130951)
XLA Ops:
  0.7 0.0 copy-start
  0.7 0.6 %copy-done = f32[1,128]{1,0:T(1,128)S(1)} copy-done((f32[1,128]{1,0:T(1,128)S(1)}, f32[1,128]{1,0:T(1,128)}, u32[]{:S(2)}) %copy-start) | copy-done | bytes 536
  1.3 34.6 %shard_map.46 = bf16[64,32,32]{2,1,0:T(8,128)(2,1)S(1)} custom-call(bf16[1,143,2,2048]{3,2,1,0:T(2,128)(2,1)} %bitcast.1, f32[1,128]{1,0:T(1,128)S(1)} %copy-done, s32[1]{0:T(128)S(6)} %copy.6.row_ref, f32[2592,128]{1,0:T(8,128)} %constant.2.clone.table_hbm), custom_call_target="tpu_custom_call" | custom-call | tf_op jit(solution)/shard_map/pallas_call | solution.py:474
  36.0 1.3 %copy.5 = bf16[64,32,32]{0,2,1:T(8,128)(2,1)} copy(bf16[64,32,32]{2,1,0:T(8,128)(2,1)S(1)} %shard_map.46) | data formatting | bytes 262144 | tf_op jit(solution)/shard_map/pallas_call | solution.py:474
Async XLA Ops:
  0.7 0.7 %copy-start = (f32[1,128]{1,0:T(1,128)S(1)}, f32[1,128]{1,0:T(1,128)}, u32[]{:S(2)}) copy-start(f32[1,128]{1,0:T(1,128)} %flags_ref.1) | copy-start | bytes 1540
